TPU v7x, 128 devices: a whole 4x4x4 slice. The times are simulated.
128 devices in a mesh: blk: 64 (over z_hi, x, y, core), head: 2 (over z_lo).
Axes of the slice: x: 4, y: 4, z: 4 (z_hi: 2, z_lo: 2; z = z_hi * 2 + z_lo), core: 2. Of those that a mesh axis runs over, the one named last changes fastest.
Arguments:
- queries: bfloat16 [8192, 2048], P(('blk', 'head')), may hold values from -9 to 9
- keys: bfloat16 [8192, 512], P(('blk', 'head')), may hold values from -6 to 6
- values: bfloat16 [8192, 512], P(('blk', 'head')), may hold values from -6 to 6
- grad_out: bfloat16 [8192, 2048], P(('blk', 'head')), may hold values from -6 to 6
- turn_ids: int32 [8192], replicated, may hold values from 0 to 255, never falling along the last dimension, each value on 1 to 256 neighbouring positions
Outputs:
- grad_queries: bfloat16 [8192, 2048], P(('blk', 'head'))
- key_gradients: bfloat16 [8192, 512], P(('blk', 'head'))
- value_gradients: bfloat16 [8192, 512], P(('blk', 'head'))
Inputs may be any that keep to these rules, and one draw needn't show every extreme that they name: `turn_ids`: turn ids never fall and start at 0; each of the 256 turns spans 1 to 256 tokens, one exactly 256.
All inputs are finite; a program needn't handle non-finite values.
Results may differ from a plain program's by a relative error of at most 0.035.
Values may be sent and summed in bfloat16 or wider, within the bound.
A program may use at most 128 MiB of HBM per device.

v0:
```python
import math

import jax
import jax.numpy as jnp
from jax import lax
from jax.sharding import PartitionSpec as P

HEAD_SIZE = 128


def visible_mask(query_pos, query_turn, key_pos, key_turn):
    causal = key_pos[None, :] <= query_pos[:, None]
    same_turn = key_turn[None, :] == query_turn[:, None]
    kept_turn = (key_turn % 2 == 0)[None, :]
    return causal & (same_turn | kept_turn)


def body(queries, keys, values, grad_out, turn_ids):
    query_here, key_here, value_here, grad_here = (
        lax.all_to_all(queries, "head", split_axis=1, concat_axis=0, tiled=True),
        lax.all_to_all(keys, "head", split_axis=1, concat_axis=0, tiled=True),
        lax.all_to_all(values, "head", split_axis=1, concat_axis=0, tiled=True),
        lax.all_to_all(grad_out, "head", split_axis=1, concat_axis=0, tiled=True),
    )
    length = query_here.shape[0]
    groups = key_here.shape[1] // HEAD_SIZE
    queries_per_group = query_here.shape[1] // key_here.shape[1]
    factor = HEAD_SIZE ** (-0.5)
    offset = lax.axis_index("blk") * length
    query_pos = offset + jnp.arange(length, dtype=jnp.int32)
    query_turn = lax.dynamic_slice_in_dim(turn_ids, offset, length)
    query_four = query_here.reshape(length, groups, queries_per_group, HEAD_SIZE)
    grad_four = grad_here.reshape(length, groups, queries_per_group, HEAD_SIZE)
    whole_keys, whole_values = (
        lax.all_gather(key_here, "blk", axis=0, tiled=True),
        lax.all_gather(value_here, "blk", axis=0, tiled=True),
    )
    tokens_all = whole_keys.shape[0]
    block_size = math.gcd(tokens_all, 512)
    block_count = tokens_all // block_size

    def key_slab(slab_index):
        begin_row = slab_index * block_size
        slab_keys = lax.dynamic_slice_in_dim(whole_keys, begin_row, block_size, 0).reshape(
            block_size, groups, HEAD_SIZE
        )
        slab_values = lax.dynamic_slice_in_dim(whole_values, begin_row, block_size, 0).reshape(
            block_size, groups, HEAD_SIZE
        )
        key_pos = begin_row + jnp.arange(block_size, dtype=jnp.int32)
        key_turn = lax.dynamic_slice_in_dim(turn_ids, begin_row, block_size)
        return (slab_keys, slab_values, visible_mask(query_pos, query_turn, key_pos, key_turn))

    def scores(slab_keys, slab_mask):
        raw_scores = (
            jnp.einsum("tgrd,bgd->grtb", query_four, slab_keys, preferred_element_type=jnp.float32)
            * factor
        )
        return jnp.where(slab_mask[None, None], raw_scores, -jnp.inf)

    def stats_step(slab_index, carried):
        running_max, running_sum = carried
        slab_keys, slab_values, slab_mask = key_slab(slab_index)
        logits = scores(slab_keys, slab_mask)
        new_max = jnp.maximum(running_max, jnp.max(logits, axis=-1))
        running_sum = running_sum * jnp.exp(running_max - new_max) + jnp.sum(
            jnp.exp(logits - new_max[..., None]), axis=-1
        )
        return (new_max, running_sum)

    start_max = jnp.full((groups, queries_per_group, length), -jnp.inf, jnp.float32)
    running_max, running_sum = lax.fori_loop(
        0, block_count, stats_step, (start_max, jnp.zeros_like(start_max))
    )
    log_total = running_max + jnp.log(running_sum)

    def output_step(slab_index, total_out):
        slab_keys, slab_values, slab_mask = key_slab(slab_index)
        weights = jnp.exp(scores(slab_keys, slab_mask) - log_total[..., None]).astype(jnp.bfloat16)
        return total_out + jnp.einsum(
            "grtb,bgd->tgrd", weights, slab_values, preferred_element_type=jnp.float32
        )

    forward_out = lax.fori_loop(
        0,
        block_count,
        output_step,
        jnp.zeros((length, groups, queries_per_group, HEAD_SIZE), jnp.float32),
    ).astype(jnp.bfloat16)
    out_dot = jnp.sum(
        grad_four.astype(jnp.float32) * forward_out.astype(jnp.float32), axis=-1
    ).transpose(1, 2, 0)

    def gradient_terms(slab_index):
        slab_keys, slab_values, slab_mask = key_slab(slab_index)
        attention = jnp.exp(scores(slab_keys, slab_mask) - log_total[..., None])
        rounded = attention.astype(jnp.bfloat16)
        grad_probs = jnp.einsum(
            "tgrd,bgd->grtb", grad_four, slab_values, preferred_element_type=jnp.float32
        )
        grad_logits = (attention * (grad_probs - out_dot[..., None])).astype(jnp.bfloat16)
        return (slab_keys, rounded, grad_logits)

    query_zeros = jnp.zeros((length, groups, queries_per_group, HEAD_SIZE), jnp.float32)

    def backward_step(slab_index, carried):
        grad_query, grad_keys_all, grad_values_all = carried
        slab_keys, rounded, grad_logits = gradient_terms(slab_index)
        grad_query = grad_query + jnp.einsum(
            "grtb,bgd->tgrd", grad_logits, slab_keys, preferred_element_type=jnp.float32
        )
        key_term = (
            jnp.einsum(
                "grtb,tgrd->bgd", grad_logits, query_four, preferred_element_type=jnp.float32
            )
            * factor
        )
        value_term = jnp.einsum(
            "grtb,tgrd->bgd", rounded, grad_four, preferred_element_type=jnp.float32
        )
        begin_row = slab_index * block_size
        grad_keys_all = lax.dynamic_update_slice_in_dim(grad_keys_all, key_term, begin_row, 0)
        grad_values_all = lax.dynamic_update_slice_in_dim(grad_values_all, value_term, begin_row, 0)
        return (grad_query, grad_keys_all, grad_values_all)

    key_zeros = jnp.zeros((tokens_all, groups, HEAD_SIZE), jnp.float32)
    grad_query, grad_keys_all, grad_values_all = lax.fori_loop(
        0, block_count, backward_step, (query_zeros, key_zeros, key_zeros)
    )
    grad_keys_own, grad_values_own = (
        lax.psum_scatter(grad_keys_all, "blk", scatter_dimension=0, tiled=True),
        lax.psum_scatter(grad_values_all, "blk", scatter_dimension=0, tiled=True),
    )
    grad_query_out = (
        (grad_query * factor)
        .astype(jnp.bfloat16)
        .reshape(length, groups * queries_per_group * HEAD_SIZE)
    )
    grad_keys_out = grad_keys_own.astype(jnp.bfloat16).reshape(length, groups * HEAD_SIZE)
    grad_values_out = grad_values_own.astype(jnp.bfloat16).reshape(length, groups * HEAD_SIZE)
    return (
        lax.all_to_all(grad_query_out, "head", split_axis=0, concat_axis=1, tiled=True),
        lax.all_to_all(grad_keys_out, "head", split_axis=0, concat_axis=1, tiled=True),
        lax.all_to_all(grad_values_out, "head", split_axis=0, concat_axis=1, tiled=True),
    )


def solution(mesh):
    in_specs = (
        P(("blk", "head"), None),
        P(("blk", "head"), None),
        P(("blk", "head"), None),
        P(("blk", "head"), None),
        P(),
    )
    out_specs = (P(("blk", "head"), None), P(("blk", "head"), None), P(("blk", "head"), None))
    return jax.shard_map(body, mesh=mesh, in_specs=in_specs, out_specs=out_specs, check_vma=False)
```

profile of v0, /device:TPU:1, one launch (start us, length us, event | category | flops | bytes accessed | tf_op | source)
XLA Modules:
  0.0 1022.6 jit_solution(4311382453712079848)
XLA Ops:
  8.1 7.0 all_to_all.127
  15.1 1.5 copy.138
  16.6 3.3 all-to-all-start.2
  19.9 1.7 copy.137
  21.5 1.3 all-to-all-done.2
  22.8 3.4 all-to-all-start.1
  26.3 1.7 copy.136
  28.0 2.3 all-to-all-done.1
  30.3 3.4 all-to-all-start.3
  34.9 3.3 all-to-all-done.3
  38.4 53.8 %all-gather.3.cloned.1.call-done = bf16[8192,256]{1,0:T(8,128)(2,1)} async-done(((bf16[128,256]{1,0:T(8,128)(2,1)}), bf16[8192,256]{1,0:T(8,128)(2,1)}) %all-gather.3.cloned.1.call-update) | async-done | bytes 4194320 | tf_op jit(solution)/shard_map/all_gather | solution.py:35
  92.2 6.4 copy.96
  98.6 49.8 %while.54 = (s32[]{:T(128)}, f32[2,4,128]{2,1,0:T(4,128)S(1)}, f32[2,4,128]{2,1,0:T(4,128)S(1)}, s32[8192]{0:T(1024)}, s32[128]{0:T(128)S(1)}, /*index=5*/bf16[8...) while((s32[]{:T(128)}, f32[2,4,128]{2,1,0:T(4,128)S(1)}, ...), condition=%wide.region_3.4_spmd.clone, body=%wide.region_0.3_spmd.clone.sunk | while | flops 138161792 | bytes 5505734 | solution.py:72
  148.4 17.6 %all-gather.5.cloned.1.call-done = bf16[8192,256]{1,0:T(8,128)(2,1)} async-done(((bf16[128,256]{1,0:T(8,128)(2,1)}), bf16[8192,256]{1,0:T(8,128)(2,1)}) %all-gather.5.cloned.1.call-update) | async-done | bytes 4194320 | tf_op jit(solution)/shard_map/all_gather | solution.py:36
  166.0 6.4 copy.98
  172.4 50.3 %while.55 = (s32[]{:T(128)}, f32[128,2,4,128]{0,3,2,1:T(8,128)S(1)}, bf16[8192,256]{0,1:T(8,128)(2,1)}, s32[8192]{0:T(1024)}, s32[128]{0:T(128)S(1)}, /*index=5*...) while((s32[]{:T(128)}, ...), condition=%wide.region_5.6_spmd.clone, body=%wide.region_4.5_spmd.clone.sunk | while | flops 271063680 | bytes 3031757 | solution.py:84
  223.5 3.8 broadcast_in_dim.166.clone
  227.2 3.8 broadcast_in_dim.166
  231.0 98.1 %while.56 = (s32[]{:T(128)}, f32[128,2,4,128]{0,3,2,1:T(8,128)S(1)}, f32[8192,2,128]{2,0,1:T(8,128)}, f32[8192,2,128]{2,0,1:T(8,128)}, bf16[8192,256]{0,1:T(8,12...) while((s32[]{:T(128)}, ...), condition=%wide.region_8.9_spmd.clone, body=%wide.region_7.8_spmd.clone.sunk | while | flops 675420800 | bytes 14570229 | solution.py:127
  234.7 1.2 fusion.101
  235.9 1.2 fusion.100
  240.8 1.2 fusion.101
  247.0 1.2 fusion.101
  253.1 1.2 fusion.101
  260.4 1.2 fusion.100
  266.5 1.2 fusion.100
  271.4 1.2 fusion.101
  272.6 1.2 fusion.100
  277.5 1.2 fusion.101
  278.8 1.2 fusion.100
  283.7 1.2 fusion.101
  289.8 1.2 fusion.101
  291.0 1.2 fusion.100
  295.9 1.2 fusion.101
  297.1 1.2 fusion.100
  302.0 1.2 fusion.101
  308.1 1.2 fusion.101
  315.5 1.2 fusion.100
  320.4 1.3 fusion.101
  321.6 1.3 fusion.100
  326.5 1.3 fusion.101
  327.8 1.3 fusion.100
  330.8 3.4 all-to-all-start.4
  334.3 330.3 %reduce-scatter.3.cloned.1.call-done = f32[128,2,128]{2,0,1:T(8,128)} async-done(((f32[8192,2,128]{2,0,1:T(8,128)}), f32[128,2,128]{2,0,1:T(8,128)}) %reduce-scatter.3.cloned.1.call-update) | async-done | bytes 131088 | tf_op jit(solution)/shard_map/reduce_scatter | solution.py:131
  666.3 3.3 all-to-all-start.5
  669.6 337.9 %reduce-scatter.5.cloned.1.call-done = f32[128,2,128]{2,0,1:T(8,128)} async-done(((f32[8192,2,128]{2,0,1:T(8,128)}), f32[128,2,128]{2,0,1:T(8,128)}) %reduce-scatter.5.cloned.1.call-update) | async-done | bytes 131088 | tf_op jit(solution)/shard_map/reduce_scatter | solution.py:132
  1009.2 3.3 all-to-all-start.6
  1013.9 1.6 all-to-all-done.6
  (431 shorter events, 177.1 us)
Async XLA Ops:
  7.2 85.0 %all-gather.3.cloned.1.call-start = ((), (), s32[]{:S(2)}) async-start(), calls=%async_computation.9 | async-start | bytes 4259840 | tf_op jit(solution)/shard_map/all_gather | solution.py:35
  16.6 6.3 all-to-all-start.2
  22.8 11.8 %copy-start = (bf16[64,2,256]{2,0,1:T(8,128)(2,1)}, bf16[64,2,256]{2,0,1:T(8,128)(2,1)S(1)}, u32[]{:S(2)}) copy-start(bf16[64,2,256]{2,0,1:T(8,128)(2,1)S(1)} %all-to-all-done.2) | copy-start | bytes 196612
  22.8 7.5 all-to-all-start.1
  30.3 7.9 all-to-all-start.3
  33.7 132.3 %all-gather.5.cloned.1.call-start = ((), (), s32[]{:S(2)}) async-start(), calls=%async_computation.10 | async-start | bytes 4259840 | tf_op jit(solution)/shard_map/all_gather | solution.py:36
  34.6 630.0 %reduce-scatter.3.cloned.1.call-start = ((), (), s32[]{:S(2)}) async-start(), calls=%async_computation.11 | async-start | bytes 8519680 | tf_op jit(solution)/shard_map/reduce_scatter | solution.py:131
  329.1 678.4 %reduce-scatter.5.cloned.1.call-start = ((), (), s32[]{:S(2)}) async-start(), calls=%async_computation.12 | async-start | bytes 8519680 | tf_op jit(solution)/shard_map/reduce_scatter | solution.py:132
  330.8 335.4 %all-to-all-start.4 = ((bf16[2,64,1024]{2,1,0:T(8,128)(2,1)}), bf16[2,64,1024]{2,1,0:T(8,128)(2,1)S(1)}, u32[]{:S(2)}, u32[]{:S(2)}) async-start(bf16[2,64,1024]{2,1,0:T(8,128)(2,1)} %all_to_all.108), calls=%async_computation.4 | async-start | bytes 524288 | tf_op jit(solution)/shard_map/all_to_all | solution.py:142
  666.3 342.9 %all-to-all-start.5 = ((bf16[2,64,256]{2,1,0:T(8,128)(2,1)}), bf16[2,64,256]{2,1,0:T(8,128)(2,1)S(1)}, u32[]{:S(2)}, u32[]{:S(2)}) async-start(bf16[2,64,256]{2,1,0:T(8,128)(2,1)} %all_to_all.112), calls=%async_computation.6 | async-start | bytes 131072 | tf_op jit(solution)/shard_map/all_to_all | solution.py:143
  1009.2 6.3 all-to-all-start.6
Sparse Core Ops, SparseCore 0:
  15.2 76.9 all-gather.2
  96.0 70.0 all-gather.4
  329.2 335.3 reduce-scatter.2
  666.8 340.6 reduce-scatter.4
where the time goes:
time: 1030 us; the launch traced here: 1020 us
  waiting for transfers between devices  749 us (73%)
  matrix products  87.5 us (8%)
  local copies, waits for them, and re-layouts  82.1 us (8%)
  other arithmetic  60.5 us (6%)
  starting transfers between devices  20.4 us (2%)
  between operations  13.9 us (1%)
    reduce_scatter x1, waiting for transfers between devices, body(): lax.psum_scatter(grad_values_all, 'blk', scatter_dimension=0, tiled=True)  338 us
    reduce_scatter x1, waiting for transfers between devices, body(): lax.psum_scatter(grad_keys_all, 'blk', scatter_dimension=0, tiled=True)  330 us
    all_gather x1, waiting for transfers between devices, body(): lax.all_gather(key_here, 'blk', axis=0, tiled=True)  53.8 us
    eq x48, other arithmetic, visible_mask(): kept_turn = (key_turn % 2 == 0)[None, :]  37.1 us
    dynamic_slice x32, local copies, waits for them, and re-layouts, key_slab(): lax.dynamic_slice_in_dim(whole_keys, begin_row, block_size, 0)  32.8 us
  transfers between devices with their start and end apart: 10, of which 8 were waited for; matrix products, arithmetic and copies ran while one was open for 6% of the time, Pallas kernels for 0%

commit v1 on v0

v1 whole, which is shorter than its diff:
```python
import functools
import math

import jax
import jax.numpy as jnp
from jax import lax
from jax.experimental import pallas as pl
from jax.experimental.pallas import tpu as pltpu
from jax.sharding import PartitionSpec as P

HEAD_SIZE = 128
CHUNK = 128
TILE = 256
TILES = 32
PER_GROUP = 4
ROWS = PER_GROUP * CHUNK
HIDDEN = -1e30
FACTOR = HEAD_SIZE**-0.5
MESH = pl.DeviceIdType.MESH


def place():
    blk = lax.axis_index("blk")
    z_lo = lax.axis_index("head")
    z_hi = lax.div(blk, 32)
    part = lax.rem(blk, 32)
    x = lax.div(part, 8)
    y = lax.rem(lax.div(part, 2), 4)
    core = lax.rem(part, 2)
    return x, y, z_hi * 2 + z_lo, z_hi, z_lo, core


def device(x, y, z, core):
    return (lax.div(z, 2) * 32 + x * 8 + y * 2 + core, lax.rem(z, 2))


def wrap(a):
    return lax.rem(a + 4, 4)


def send(src, dst, send_sem, recv_sem, target):
    return pltpu.make_async_remote_copy(
        src_ref=src,
        dst_ref=dst,
        send_sem=send_sem,
        recv_sem=recv_sem,
        device_id=target,
        device_id_type=MESH,
    )


def arrived(ref, sem):
    pltpu.make_async_copy(ref, ref, sem).wait()


def greet(x, y, z, core):
    others = []
    for r in range(4):
        other_z = lax.rem(z + r, 4)
        if r:
            others.append(device(x, y, other_z, core))
        others.append(device(x, y, other_z, 1 - core))
        others.append(device(3 - x, 3 - y, other_z, 1 - core))
    for step in (-1, 1):
        others.append(device(wrap(x + step), y, z, core))
        others.append(device(x, wrap(y + step), z, core))
    barrier = pltpu.get_barrier_semaphore()
    for other in others:
        pl.semaphore_signal(barrier, inc=1, device_id=other, device_id_type=MESH)
    pl.semaphore_wait(barrier, len(others))


def plane(x, y, z, core):
    first, second = x + core * (y - x), y + core * (x - y)

    def index(i, j):
        return (i + core * (j - i)) * 4 + j + core * (i - j)

    def target(i, j):
        return device(i + core * (j - i), j + core * (i - j), z, core)

    return first, second, index, target


def gather_kernel(
    q_ref, k_ref, v_ref, o_ref, kv_ref, qs_ref, os_ref,
    kv_send, kv_recv, qo_send, qo_recv, first_send, first_recv, second_send, second_recv, twin_send, twin_recv,
):
    x, y, z, z_hi, z_lo, core = place()
    first, second, index, target = plane(x, y, z, core)
    greet(x, y, z, core)
    here = x * 4 + y
    rows = pl.ds(pl.multiple_of(core * 128 + z_lo * 64, 64), 64)

    waits = []
    for r in (1, 3, 2, 0):
        other_z = lax.rem(z + r, 4)
        columns = pl.ds(pl.multiple_of(other_z * 128, 128), 128)
        for role, ref in ((0, k_ref), (1, v_ref)):
            dst = kv_ref.at[role, here, z_hi, rows]
            src = ref.at[:, columns]
            copy = send(
                src, dst, kv_send.at[role, r], kv_recv.at[z, core], device(x, y, other_z, role)
            )
            if r:
                copy.start()
                waits.append(copy)
            else:

                @pl.when(core == role)
                def _():
                    pltpu.make_async_copy(src, dst, kv_recv.at[z, core]).start()

                @pl.when(core != role)
                def _():
                    copy.start()

    mirror_x, mirror_y = x + z_hi * (3 - 2 * x), y + z_hi * (3 - 2 * y)
    mirror_core = core + z_hi * (1 - 2 * core)
    own_rows = pl.ds(pl.multiple_of(z_lo * 64, 64), 64)
    for r in (2, 1, 3, 0):
        other_z = lax.rem(z + r, 4)
        columns = pl.ds(pl.multiple_of(other_z * 512, 512), 512)
        for role, ref, out in ((0, q_ref, qs_ref), (1, o_ref, os_ref)):
            src, dst = ref.at[:, columns], out.at[z_hi, own_rows]
            copy = send(
                src, dst, qo_send.at[role, r], qo_recv.at[role, z],
                device(mirror_x, mirror_y, other_z, mirror_core),
            )
            if r:
                copy.start()
                waits.append(copy)
            else:

                @pl.when(z_hi == 0)
                def _():
                    pltpu.make_async_copy(src, dst, qo_recv.at[role, z]).start()

                @pl.when(z_hi == 1)
                def _():
                    copy.start()

    def block(i, j):
        return kv_ref.at[core, index(i, j)]

    def half(i, j, h):
        return kv_ref.at[core, index(i, j), h]

    def go(src, send_sem, recv_sem, to):
        copy = send(src, src, send_sem, recv_sem, to)
        copy.start()
        waits.append(copy)

    up, down = wrap(first + 1), wrap(first - 1)
    left, right = wrap(second - 1), wrap(second + 1)
    order = (first, down, up, wrap(first + 2))

    def twin(i, j, slot):
        go(block(i, j), twin_send.at[slot], twin_recv.at[slot], device(x, y, z, 1 - core))

    def spread(k):
        i = order[k]
        go(block(i, second), second_send.at[k, 0], second_recv.at[k, 0], target(first, right))
        go(block(i, second), second_send.at[k, 1], second_recv.at[k, 1], target(first, left))
        twin(i, second, 4 * k)

    def second_hop(k):
        i = order[k]
        arrived(block(i, left), second_recv.at[k, 0])
        go(half(i, left, 0), second_send.at[k, 2], second_recv.at[k, 2], target(first, right))
        twin(i, left, 4 * k + 1)
        arrived(block(i, right), second_recv.at[k, 1])
        go(half(i, right, 1), second_send.at[k, 3], second_recv.at[k, 3], target(first, left))
        twin(i, right, 4 * k + 2)

    def last_hop(k):
        i, j = order[k], wrap(second + 2)
        arrived(half(i, j, 0), second_recv.at[k, 2])
        arrived(half(i, j, 1), second_recv.at[k, 3])
        twin(i, j, 4 * k + 3)

    for other_z in range(4):
        for other_core in range(2):
            arrived(
                kv_ref.at[core, here, other_z // 2, pl.ds(other_core * 128 + (other_z % 2) * 64, 64)],
                kv_recv.at[other_z, other_core],
            )
    go(block(first, second), first_send.at[0], first_recv.at[0], target(up, second))
    go(block(first, second), first_send.at[1], first_recv.at[1], target(down, second))
    spread(0)
    arrived(block(down, second), first_recv.at[0])
    go(half(down, second, 0), first_send.at[2], first_recv.at[2], target(up, second))
    spread(1)
    arrived(block(up, second), first_recv.at[1])
    go(half(up, second, 1), first_send.at[3], first_recv.at[3], target(down, second))
    spread(2)
    second_hop(0)
    arrived(half(order[3], second, 0), first_recv.at[2])
    arrived(half(order[3], second, 1), first_recv.at[3])
    spread(3)
    second_hop(1)
    second_hop(2)
    last_hop(0)
    second_hop(3)
    last_hop(1)
    last_hop(2)
    last_hop(3)

    for slot in range(16):
        arrived(kv_ref.at[1 - core, slot], twin_recv.at[slot])
    for role, out in ((0, qs_ref), (1, os_ref)):
        for other_z in range(4):
            arrived(
                out.at[other_z // 2, pl.ds((other_z % 2) * 64, 64)], qo_recv.at[role, other_z]
            )
    for copy in waits:
        copy.wait_send()
    for role, ref in ((0, k_ref), (1, v_ref)):

        @pl.when(core != role)
        def _():
            src = ref.at[:, pl.ds(0, 128)]
            pltpu.make_async_copy(src, src, kv_send.at[role, 0]).wait()

    for role, ref in ((0, q_ref), (1, o_ref)):

        @pl.when(z_hi == 1)
        def _():
            src = ref.at[:, pl.ds(0, 512)]
            pltpu.make_async_copy(src, src, qo_send.at[role, 0]).wait()


def attention_kernel(
    place_ref, turn_ref, query_turn_ref, kv_ref, q_ref, o_ref, dkv_ref, dq_ref,
    qs, os, weights, probs_grad, tile_max, dq_acc,
):
    part = place_ref[0]
    chunks = (part, 63 - part)
    counts = (lax.div(part, 2) + 1, lax.div(63 - part, 2) + 1)
    starts = (0, counts[0])
    scale = FACTOR * math.log2(math.e)

    for s in range(2):
        for h in range(PER_GROUP):
            lanes, lines = pl.ds(h * 128, 128), pl.ds(h * CHUNK, CHUNK)
            qs[s, lines, :] = q_ref[s, :, lanes]
            os[s, lines, :] = o_ref[s, :, lanes]

    def stored(t):
        return lax.rem(t, 16) * 2 + lax.div(t, 16)

    finals = []
    for s in range(2):
        query_pos = chunks[s] * CHUNK + lax.broadcasted_iota(jnp.int32, (1, CHUNK), 1)
        query_turn = query_turn_ref[pl.ds(chunks[s], 1), :]

        def stats(t, carried, s=s, query_pos=query_pos, query_turn=query_turn):
            top, total, dot = carried
            at = stored(t)
            key_turn = jnp.broadcast_to(turn_ref[pl.ds(t, 1), :], (CHUNK, TILE)).T
            key_pos = t * TILE + lax.broadcasted_iota(jnp.int32, (TILE, CHUNK), 0)
            visible = (key_pos <= query_pos) & (
                (key_turn == query_turn) | ((key_turn & 1) == 0)
            )
            logits = lax.dot_general(
                kv_ref[0, at], qs[s], (((1,), (1,)), ((), ())), preferred_element_type=jnp.float32
            )
            bias = jnp.where(visible, 0.0, HIDDEN)
            logits = logits * scale + jnp.concatenate([bias] * PER_GROUP, axis=1)
            new_top = jnp.maximum(top, jnp.max(logits, axis=0, keepdims=True))
            shrink = jnp.exp2(top - new_top)
            weight = jnp.exp2(logits - new_top)
            grads = lax.dot_general(
                kv_ref[1, at], os[s], (((1,), (1,)), ((), ())), preferred_element_type=jnp.float32
            )
            item = starts[s] + t
            weights[item] = weight.astype(jnp.bfloat16)
            probs_grad[item] = grads.astype(jnp.bfloat16)
            tile_max[pl.ds(item, 1), :] = new_top
            total = total * shrink + jnp.sum(weight, axis=0, keepdims=True)
            dot = dot * shrink + jnp.sum(weight * grads, axis=0, keepdims=True)
            return new_top, total, dot

        zero = jnp.zeros((1, ROWS), jnp.float32)
        top, total, dot = lax.fori_loop(
            0, counts[s], stats, (jnp.full((1, ROWS), HIDDEN, jnp.float32), zero, zero)
        )
        share = 1.0 / total
        finals.append((top, share, dot * share))

    dq_acc[...] = jnp.zeros_like(dq_acc)

    def terms(s, t):
        item = starts[s] + t
        top, share, dot = finals[s]
        by = jnp.exp2(tile_max[pl.ds(item, 1), :] - top) * share
        attention = weights[item].astype(jnp.float32) * by
        logit_grad = (attention * (probs_grad[item].astype(jnp.float32) - dot)).astype(jnp.bfloat16)
        value_term = jnp.dot(
            attention.astype(jnp.bfloat16), os[s], preferred_element_type=jnp.float32
        )
        key_term = jnp.dot(logit_grad, qs[s], preferred_element_type=jnp.float32)
        dq_acc[s] += lax.dot_general(
            logit_grad, kv_ref[0, stored(t)], (((0,), (0,)), ((), ())),
            preferred_element_type=jnp.float32,
        )
        return key_term, value_term

    def both(t, _):
        key_a, value_a = terms(0, t)
        key_b, value_b = terms(1, t)
        at = stored(t)
        dkv_ref[0, at] = ((key_a + key_b) * FACTOR).astype(jnp.bfloat16)
        dkv_ref[1, at] = (value_a + value_b).astype(jnp.bfloat16)
        return 0

    def late(t, _):
        key_b, value_b = terms(1, t)
        at = stored(t)
        dkv_ref[0, at] = (key_b * FACTOR).astype(jnp.bfloat16)
        dkv_ref[1, at] = value_b.astype(jnp.bfloat16)
        return 0

    def unseen(t, _):
        at = stored(t)
        empty = jnp.zeros((TILE, HEAD_SIZE), jnp.bfloat16)
        dkv_ref[0, at] = empty
        dkv_ref[1, at] = empty
        return 0

    lax.fori_loop(0, counts[0], both, 0)
    lax.fori_loop(counts[0], counts[1], late, 0)
    lax.fori_loop(counts[1], TILES, unseen, 0)
    for s in range(2):
        for h in range(PER_GROUP):
            dq_ref[s, :, pl.ds(h * 128, 128)] = (
                dq_acc[s, pl.ds(h * CHUNK, CHUNK), :] * FACTOR
            ).astype(jnp.bfloat16)


def reduce_kernel(
    g_ref, dq_ref, dq_out, dkv_out,
    twin, total, one, two, line, one_f, two_f, done,
    twin_send, twin_recv, second_send, second_recv, first_send, first_recv,
    kv_send, kv_recv, dq_send, dq_recv,
):
    x, y, z, z_hi, z_lo, core = place()
    first, second, index, target = plane(x, y, z, core)
    greet(x, y, z, core)
    waits = []

    def go(src, dst, send_sem, recv_sem, to):
        copy = send(src, dst, send_sem, recv_sem, to)
        copy.start()
        waits.append(copy)

    def orders(f, s):
        return (
            (wrap(f + 2), wrap(f + 1), wrap(f - 1), f),
            (wrap(s + 2), wrap(s + 1), wrap(s - 1), s),
        )

    other_i, other_j = orders(second, first)
    for b in range(4):
        for a in range(4):
            at = index(other_j[b], other_i[a])
            slot = 4 * b + a
            go(g_ref.at[1 - core, at], twin.at[at], twin_send.at[slot], twin_recv.at[slot],
               device(x, y, z, 1 - core))

    for other_z in range(4):
        other_hi, other_lo = other_z // 2, other_z % 2
        tx, ty, tc = (3 - x, 3 - y, 1 - core) if other_hi else (x, y, core)
        src = dq_ref.at[other_hi, pl.ds(other_lo * 64, 64)]
        dst = dq_out.at[:, pl.ds(pl.multiple_of(z * 512, 512), 512)]
        copy = send(src, dst, dq_send.at[other_z], dq_recv.at[z], device(tx, ty, other_z, tc))
        if other_hi:
            copy.start()
            waits.append(copy)
        else:

            @pl.when(z == other_z)
            def _():
                pltpu.make_async_copy(src, dst, dq_recv.at[z]).start()

            @pl.when(z != other_z)
            def _():
                copy.start()

    order, across = orders(first, second)
    right, left = across[1], across[2]
    up, down = order[1], order[2]

    def chip_sum(i, j, a, b):
        at = index(i, j)
        arrived(twin.at[at], twin_recv.at[4 * b + a])
        return g_ref[core, at].astype(jnp.float32) + twin[at].astype(jnp.float32)

    for a in range(4):
        i, j = order[a], across[0]
        at = index(i, j)
        total[a, 0] = chip_sum(i, j, a, 0).astype(jnp.bfloat16)
        go(total.at[a, 0, 0], one.at[a, 0], second_send.at[a, 0], second_recv.at[a, 0], target(first, right))
        go(total.at[a, 0, 1], one.at[a, 1], second_send.at[a, 1], second_recv.at[a, 1], target(first, left))
    for a in range(4):
        i = order[a]
        for b, to in ((1, right), (2, left)):
            h = b - 1
            value = chip_sum(i, across[b], a, b)
            arrived(one.at[a, h], second_recv.at[a, h])
            total[a, b, 1 - h] = value[1 - h].astype(jnp.bfloat16)
            total[a, b, h] = (value[h] + one[a, h].astype(jnp.float32)).astype(jnp.bfloat16)
            go(total.at[a, b], two.at[a, h], second_send.at[a, 2 + h], second_recv.at[a, 2 + h], target(first, to))
    for a in range(4):
        i = order[a]
        value = chip_sum(i, second, a, 3)
        arrived(two.at[a, 0], second_recv.at[a, 2])
        arrived(two.at[a, 1], second_recv.at[a, 3])
        value = value + two[a, 0].astype(jnp.float32) + two[a, 1].astype(jnp.float32)
        if a == 0:
            line[0] = value.astype(jnp.bfloat16)
            go(line.at[0, 0], one_f.at[0], first_send.at[0], first_recv.at[0], target(up, second))
            go(line.at[0, 1], one_f.at[1], first_send.at[1], first_recv.at[1], target(down, second))
        elif a < 3:
            h = a - 1
            arrived(one_f.at[h], first_recv.at[h])
            line[a, 1 - h] = value[1 - h].astype(jnp.bfloat16)
            line[a, h] = (value[h] + one_f[h].astype(jnp.float32)).astype(jnp.bfloat16)
            go(line.at[a], two_f.at[h], first_send.at[2 + h], first_recv.at[2 + h],
               target(up if a == 1 else down, second))
        else:
            arrived(two_f.at[0], first_recv.at[2])
            arrived(two_f.at[1], first_recv.at[3])
            value = value + two_f[0].astype(jnp.float32) + two_f[1].astype(jnp.float32)
            done[...] = value.astype(jnp.bfloat16)

    for other_z in range(4):
        for other_core in range(2):
            src = done.at[other_z // 2, pl.ds(other_core * 128 + (other_z % 2) * 64, 64)]
            dst = dkv_out.at[core, :, pl.ds(pl.multiple_of(z * 128, 128), 128)]
            slot = kv_recv.at[core, z]
            copy = send(src, dst, kv_send.at[other_z, other_core], slot, device(x, y, other_z, other_core))
            own = (z == other_z) & (core == other_core)

            @pl.when(own)
            def _():
                pltpu.make_async_copy(src, dst, slot).start()

            @pl.when(jnp.logical_not(own))
            def _():
                copy.start()

    for role in range(2):
        for other_z in range(4):
            arrived(dkv_out.at[role, :, pl.ds(other_z * 128, 128)], kv_recv.at[role, other_z])
    for other_z in range(4):
        arrived(dq_out.at[:, pl.ds(other_z * 512, 512)], dq_recv.at[other_z])
    for copy in waits:
        copy.wait_send()
    for other_z in range(4):
        for other_core in range(2):

            @pl.when(jnp.logical_not((z == other_z) & (core == other_core)))
            def _():
                arrived(done.at[0, pl.ds(0, 64)], kv_send.at[other_z, other_core])

    for other_z in range(2):

        @pl.when(z != other_z)
        def _():
            arrived(dq_ref.at[0, pl.ds(0, 64)], dq_send.at[other_z])


ANY = pl.BlockSpec(memory_space=pl.ANY)
VMEM = pl.BlockSpec(memory_space=pltpu.VMEM)
SMEM = pl.BlockSpec(memory_space=pltpu.SMEM)
BF16 = jnp.bfloat16
DMA = pltpu.SemaphoreType.DMA


def exchange(queries, keys, values, grad_out):
    return pl.pallas_call(
        gather_kernel,
        out_shape=(
            jax.ShapeDtypeStruct((2, 16, 2, 256, 128), BF16),
            jax.ShapeDtypeStruct((2, CHUNK, 512), BF16),
            jax.ShapeDtypeStruct((2, CHUNK, 512), BF16),
        ),
        in_specs=[ANY] * 4,
        out_specs=(VMEM, ANY, ANY),
        scratch_shapes=[
            DMA((2, 4)), DMA((4, 2)),
            DMA((2, 4)), DMA((2, 4)),
            DMA((4,)), DMA((4,)),
            DMA((4, 4)), DMA((4, 4)),
            DMA((16,)), DMA((16,)),
        ],
        compiler_params=pltpu.CompilerParams(
            collective_id=0, has_side_effects=True, vmem_limit_bytes=32 << 20
        ),
        name="exchange",
    )(queries, keys, values, grad_out)


def attend(part, turn_ids, kv, queries, grads):
    return pl.pallas_call(
        attention_kernel,
        out_shape=(
            jax.ShapeDtypeStruct((2, TILES, TILE, 128), BF16),
            jax.ShapeDtypeStruct((2, CHUNK, 512), BF16),
        ),
        in_specs=[SMEM] + [VMEM] * 5,
        out_specs=(VMEM, VMEM),
        scratch_shapes=[
            pltpu.VMEM((2, ROWS, 128), BF16),
            pltpu.VMEM((2, ROWS, 128), BF16),
            pltpu.VMEM((33, TILE, ROWS), BF16),
            pltpu.VMEM((33, TILE, ROWS), BF16),
            pltpu.VMEM((33, ROWS), jnp.float32),
            pltpu.VMEM((2, ROWS, 128), jnp.float32),
        ],
        compiler_params=pltpu.CompilerParams(vmem_limit_bytes=56 << 20),
        name="attend",
    )(part, turn_ids.reshape(TILES, TILE), turn_ids.reshape(64, CHUNK), kv, queries, grads)


def combine(partial, dq):
    half = (256, 128)
    whole = (2, 256, 128)
    return pl.pallas_call(
        reduce_kernel,
        out_shape=(
            jax.ShapeDtypeStruct((64, 2048), BF16),
            jax.ShapeDtypeStruct((2, 64, 512), BF16),
        ),
        in_specs=[VMEM, ANY],
        out_specs=(ANY, ANY),
        scratch_shapes=[
            pltpu.VMEM((16,) + whole, BF16),
            pltpu.VMEM((4, 3) + whole, BF16),
            pltpu.VMEM((4, 2) + half, BF16),
            pltpu.VMEM((4, 2) + whole, BF16),
            pltpu.VMEM((3,) + whole, BF16),
            pltpu.VMEM((2,) + half, BF16),
            pltpu.VMEM((2,) + whole, BF16),
            pltpu.VMEM(whole, BF16),
            DMA((16,)), DMA((16,)),
            DMA((4, 4)), DMA((4, 4)),
            DMA((4,)), DMA((4,)),
            DMA((4, 2)), DMA((2, 4)),
            DMA((4,)), DMA((4,)),
        ],
        compiler_params=pltpu.CompilerParams(
            collective_id=1, has_side_effects=True, vmem_limit_bytes=40 << 20
        ),
        name="combine",
    )(partial, dq)


def body(queries, keys, values, grad_out, turn_ids):
    kv, own_queries, own_grads = exchange(queries, keys, values, grad_out)
    part = lax.rem(lax.axis_index("blk"), 32).astype(jnp.int32).reshape(1)
    partial, dq = attend(part, turn_ids, kv.reshape(2, TILES, TILE, 128), own_queries, own_grads)
    dq_out, dkv_out = combine(partial.reshape(2, 16, 2, 256, 128), dq)
    return dq_out, dkv_out[0], dkv_out[1]


def solution(mesh):
    spread = P(("blk", "head"), None)
    return jax.shard_map(
        body,
        mesh=mesh,
        in_specs=(spread,) * 4 + (P(),),
        out_specs=(spread,) * 3,
        check_vma=False,
    )
```

time: 1030 us -> 107 us (0.10)
  waiting for transfers between devices: 749 us -> 0 us
  Pallas kernels: 0 us -> 93.1 us
  matrix products: 87.5 us -> 0 us
  local copies, waits for them, and re-layouts: 82.1 us -> 12.8 us
  other arithmetic: 60.5 us -> 0 us
  starting transfers between devices: 20.4 us -> 0 us
  between operations: 13.9 us -> 0.67 us
    reduce_scatter x2 -> x0, waiting for transfers between devices: 668 us -> none  [the longest x1 338 us: body(): lax.psum_scatter(grad_values_all, 'blk', scatter_dimension=0, tiled=True)]
    pallas_call x0 -> x3, Pallas kernels: none -> 93.1 us  [the longest x1 37.3 us: exchange(): pl.pallas_call(gather_kernel, out_shape=(jax.ShapeDtypeStruct((2, 16, 2,...]
    dot_general x112 -> x0, matrix products: 87.5 us -> none  [the longest x16 19.8 us: backward_step(): jnp.einsum('grtb,tgrd->bgd', rounded, grad_four, preferred_element_type=j...]
    all_gather x2 -> x0, waiting for transfers between devices: 71.4 us -> none  [the longest x1 53.8 us: body(): lax.all_gather(key_here, 'blk', axis=0, tiled=True)]
    dynamic_slice x49 -> x0, local copies, waits for them, and re-layouts: 50.7 us -> none  [the longest x32 32.8 us: key_slab(): lax.dynamic_slice_in_dim(whole_keys, begin_row, block_size, 0)]
    eq x48 -> x0, other arithmetic: 37.1 us -> none  [visible_mask(): kept_turn = (key_turn % 2 == 0)[None, :]]
    all_to_all x6 -> x0, starting transfers between devices: 20.2 us -> none  [the longest x1 3.44 us: body(): lax.all_to_all(queries, 'head', split_axis=1, concat_axis=0, tiled=True)]
    and x48 -> x0, other arithmetic: 13 us -> none  [visible_mask(): return causal & (same_turn | kept_turn)]
  transfers between devices with their start and end apart: 10 -> 0, of which waited for: 8 -> 0; matrix products, arithmetic and copies ran while one was open for 6% -> 0% of each run, Pallas kernels for 0% -> 0%
where the time goes in v1:
time: 107 us
  Pallas kernels  93.1 us (87%)
  local copies, waits for them, and re-layouts  12.8 us (12%)
    pallas_call x1, Pallas kernels, exchange(): pl.pallas_call(gather_kernel, out_shape=(jax.ShapeDtypeStruct((2, 16, 2,...  37.3 us
    pallas_call x1, Pallas kernels, attend(): pl.pallas_call(attention_kernel, out_shape=(jax.ShapeDtypeStruct((2, TILE...  29.1 us
    pallas_call x1, Pallas kernels, combine(): pl.pallas_call(reduce_kernel, out_shape=(jax.ShapeDtypeStruct((64, 2048),...  26.7 us
    unnamed x19, local copies, waits for them, and re-layouts  10.8 us

profile of v1, /device:TPU:1, one launch (start us, length us, event | category | flops | bytes accessed | tf_op | source)
XLA Modules:
  0.0 106.6 jit_solution(888256335745539776)
XLA Ops:
  0.6 1.4 %reshape.22.turn_ref = s32[32,256]{1,0:T(8,128)} reshape(s32[8192]{0:T(1024)} %param.9) | data formatting | bytes 65536 | tf_op jit(solution)/shard_map/reshape | solution.py:524
  2.0 0.0 copy-start.5
  2.0 0.9 copy-done.5
  3.0 0.0 copy-start.6
  3.0 0.9 copy-done.6
  3.9 0.0 copy-start.7
  3.9 0.8 copy-done.7
  4.8 0.0 copy-start.8
  4.8 0.8 copy-done.8
  5.6 37.3 %exchange.1 = (bf16[2,16,2,256,128]{4,3,2,1,0:T(8,128)(2,1)S(1)}, bf16[2,128,512]{2,1,0:T(8,128)(2,1)S(1)}, bf16[2,128,512]{2,1,0:T(8,128)(2,1)S(1)}) custom-call(bf16[64,2048]{1,0:T(8,128)(2,1)S(1)} %copy-done.5, bf16[64,512]{1,0:T(8,128)(2,1)S(1)} %copy-done.7, bf16[64,512]{1,0:T(8,128)(2,1)S(1)} %copy-done.8, bf16[64,2048]{1,0:T(8,128)(2,1)S(1)} %copy-done.6), custom_call_target="tpu_custom_call" | custom-call | tf_op jit(solution)/shard_map/exchange/pallas_call | solution.py:482
  42.9 0.0 copy-start
  43.0 1.9 %copy-done = bf16[2,16,2,256,128]{4,3,2,1,0:T(8,128)(2,1)} copy-done((bf16[2,16,2,256,128]{4,3,2,1,0:T(8,128)(2,1)}, bf16[2,16,2,256,128]{4,3,2,1,0:T(8,128)(2,1)S(1)}, u32[]{:S(2)}) %copy-start) | copy-done | bytes 4194328
  44.9 0.0 copy-start.3
  44.9 0.7 copy-done.3
  45.6 0.0 copy-start.4
  45.6 0.7 copy-done.4
  46.3 29.1 %attend.1 = (bf16[2,32,256,128]{3,2,1,0:T(8,128)(2,1)}, bf16[2,128,512]{2,1,0:T(8,128)(2,1)}) custom-call(s32[1]{0:T(128)} %bitcast.place_ref, s32[32,256]{1,0:T(8,128)} %reshape.22.turn_ref, s32[64,128]{1,0:T(8,128)} %bitcast.10, bf16[2,32,256,128]{3,2,1,0:T(8,128)(2,1)} %bitcast.8, bf16[2,128,512]{2,1,0:T(8,128)(2,1)} %copy-done.3, ...), custom_call_target="tpu_custom_call" | custom-call | tf_op jit(solution)/shard_map/attend/pallas_call | solution.py:506
  75.4 0.0 copy-start.1
  75.4 2.2 %copy-done.1 = bf16[2,32,256,128]{3,2,1,0:T(8,128)(2,1)S(1)} copy-done((bf16[2,32,256,128]{3,2,1,0:T(8,128)(2,1)S(1)}, bf16[2,32,256,128]{3,2,1,0:T(8,128)(2,1)}, u32[]{:S(2)}) %copy-start.1) | copy-done | bytes 4194328
  77.6 0.0 copy-start.2
  77.6 0.9 copy-done.2
  78.6 26.7 %combine.1 = (bf16[64,2048]{1,0:T(8,128)(2,1)S(1)}, bf16[2,64,512]{2,1,0:T(8,128)(2,1)S(1)}) custom-call(bf16[2,16,2,256,128]{4,3,2,1,0:T(8,128)(2,1)S(1)} %bitcast.9, bf16[2,128,512]{2,1,0:T(8,128)(2,1)S(1)} %copy-done.2), custom_call_target="tpu_custom_call" | custom-call | tf_op jit(solution)/shard_map/combine/pallas_call | solution.py:530
  105.3 0.7 slice_bitcast_fusion
  105.9 0.7 copy.9
Async XLA Ops:
  2.0 0.9 copy-start.5
  3.0 0.9 copy-start.6
  3.9 0.8 copy-start.7
  4.8 0.8 copy-start.8
  42.9 2.0 %copy-start = (bf16[2,16,2,256,128]{4,3,2,1,0:T(8,128)(2,1)}, bf16[2,16,2,256,128]{4,3,2,1,0:T(8,128)(2,1)S(1)}, u32[]{:S(2)}) copy-start(bf16[2,16,2,256,128]{4,3,2,1,0:T(8,128)(2,1)S(1)} %get-tuple-element.10) | copy-start | bytes 12582916
  44.9 0.7 copy-start.3
  45.6 0.7 copy-start.4
  75.4 2.2 %copy-start.1 = (bf16[2,32,256,128]{3,2,1,0:T(8,128)(2,1)S(1)}, bf16[2,32,256,128]{3,2,1,0:T(8,128)(2,1)}, u32[]{:S(2)}) copy-start(bf16[2,32,256,128]{3,2,1,0:T(8,128)(2,1)} %get-tuple-element.13) | copy-start | bytes 12582916
  77.6 0.9 copy-start.2

commit v2 on v0

v2 whole, which is shorter than its diff:
```python
import math

import jax
import jax.numpy as jnp
from jax import lax
from jax.experimental import pallas as pl
from jax.experimental.pallas import tpu as pltpu
from jax.sharding import PartitionSpec as P

HEAD_SIZE = 128
CHUNK = 128
TILE = 256
PER_GROUP = 4
ROWS = PER_GROUP * CHUNK
ITEMS = 33
HIDDEN = -1e30
FACTOR = HEAD_SIZE**-0.5
BF16 = jnp.bfloat16
F32 = jnp.float32
MESH = pl.DeviceIdType.MESH

NEAR_FIRST = (
    (0, 0), (-1, 0), (1, 0), (0, -1), (0, 1), (-1, -1), (-1, 1), (1, -1), (1, 1),
    (2, 0), (0, 2), (2, -1), (2, 1), (-1, 2), (1, 2), (2, 2),
)
FAR_FIRST = (
    (2, 2), (1, 2), (-1, 2), (2, 1), (2, -1), (0, 2), (2, 0), (0, 1), (0, -1), (1, 0), (-1, 0),
    (1, 1), (1, -1), (-1, 1), (-1, -1), (0, 0),
)


def device(x, y, z, core):
    return (lax.div(z, 2) * 32 + x * 8 + y * 2 + core, lax.rem(z, 2))


def wrap(a):
    return lax.rem(a + 4, 4)


def send(src, dst, send_sem, recv_sem, target):
    return pltpu.make_async_remote_copy(
        src_ref=src,
        dst_ref=dst,
        send_sem=send_sem,
        recv_sem=recv_sem,
        device_id=target,
        device_id_type=MESH,
    )


def arrived(ref, sem):
    pltpu.make_async_copy(ref, ref, sem).wait()


def greet(x, y, z, core):
    others = []
    for r in range(4):
        other_z = lax.rem(z + r, 4)
        if r:
            others.append(device(x, y, other_z, core))
        others.append(device(x, y, other_z, 1 - core))
        others.append(device(3 - x, 3 - y, other_z, 1 - core))
        for step in (1, 2, 3):
            others.append(device(wrap(x + step), y, other_z, 0))
            others.append(device(wrap(x + step), y, other_z, 1))
            others.append(device(x, wrap(y + step), other_z, 0))
            others.append(device(x, wrap(y + step), other_z, 1))
    barrier = pltpu.get_barrier_semaphore()
    for other in others:
        pl.semaphore_signal(barrier, inc=1, device_id=other, device_id_type=MESH)
    pl.semaphore_wait(barrier, len(others))


def codes(order, axis):
    digits = [step[axis] % 4 for step in order]
    return [sum(digit * 4**i for i, digit in enumerate(digits[at : at + 8])) for at in (0, 8)]


def at_most(a, b):
    return lax.div(b - a + 16, 16)


def kernel(
    turn_ref, q_ref, k_ref, v_ref, o_ref, dq_out, dk_out, dv_out,
    kv, landed, qs, os, weights, probs_grad, tile_max, top, total, dot, dq_acc, dq_own,
    term, partial, twin, sums, one, two, line, last,
    kv_send, kv_recv, qo_send, qo_recv, first_send, first_recv, second_send, second_recv,
    twin_send, twin_recv, back_send, back_recv, ring_send, ring_recv, last_send, last_recv,
    dq_send, dq_recv,
):
    blk = lax.axis_index("blk")
    z_lo = lax.axis_index("head")
    z_hi = lax.div(blk, 32)
    part = lax.rem(blk, 32)
    x = lax.div(part, 8)
    y = lax.rem(lax.div(part, 2), 4)
    core = lax.rem(part, 2)
    z = z_hi * 2 + z_lo
    here = x * 4 + y
    first, second = x + core * (y - x), y + core * (x - y)

    def index(i, j):
        return (i + core * (j - i)) * 4 + j + core * (i - j)

    def target(i, j):
        return device(i + core * (j - i), j + core * (i - j), z, core)

    other_core = device(x, y, z, 1 - core)
    odd = lax.rem(z, 2)
    my_part = part + odd * (31 - 2 * part)
    my_block = lax.div(my_part, 2)

    greet(x, y, z, core)

    def go(src, dst, send_sem, recv_sem, to):
        send(src, dst, send_sem, recv_sem, to).start()

    def go_or_keep(own, src, dst, send_sem, recv_sem, to):
        @pl.when(own)
        def _():
            pltpu.make_async_copy(src, dst, recv_sem).start()

        @pl.when(jnp.logical_not(own))
        def _():
            send(src, dst, send_sem, recv_sem, to).start()

    rows = pl.ds(pl.multiple_of(core * 128 + z_lo * 64, 64), 64)
    for r in (2, 1, 3, 0):
        other_z = lax.rem(z + r, 4)
        columns = pl.ds(pl.multiple_of(other_z * 128, 128), 128)
        for role, ref in ((0, k_ref), (1, v_ref)):
            dst = kv.at[role, here, z_hi, rows]
            args = (ref.at[:, columns], dst, kv_send.at[role, r], kv_recv.at[z, core])
            if r:
                go(*args, device(x, y, other_z, role))
            else:
                go_or_keep(core == role, *args, device(x, y, z, role))

    own_rows = pl.ds(pl.multiple_of(z_lo * 64, 64), 64)
    for r in (2, 1, 3, 0):
        other_z = lax.rem(z + r, 4)
        flip = lax.rem(z_hi + other_z, 2)
        to = device(x + flip * (3 - 2 * x), y + flip * (3 - 2 * y), other_z, core + flip * (1 - 2 * core))
        columns = pl.ds(pl.multiple_of(other_z * 512, 512), 512)
        for role, ref in ((0, q_ref), (1, o_ref)):
            args = (ref.at[:, columns], landed.at[role, z_hi, own_rows], qo_send.at[role, r], qo_recv.at[role, z])
            if r:
                go(*args, to)
            else:
                go_or_keep(flip == 0, *args, to)

    up, down = wrap(first + 1), wrap(first - 1)
    left, right = wrap(second - 1), wrap(second + 1)
    firsts = (first, down, up, wrap(first + 2))
    steps = (0, -1, 1, 2)
    near = {step: n for n, step in enumerate(NEAR_FIRST)}
    far = {step: n for n, step in enumerate(FAR_FIRST)}

    def slot_of(table, a, b):
        return table[a, b] + core * (table[b, a] - table[a, b])

    def block(i, j):
        return kv.at[core, index(i, j)]

    def half(i, j, h):
        return kv.at[core, index(i, j), h]

    def share(i, j, a, b):
        slot = slot_of(near, a, b)
        go(block(i, j), block(i, j), twin_send.at[slot], twin_recv.at[slot], other_core)

    def relay(src, sems, to):
        go(src, src, *sems, to)

    def spread(k):
        i = firsts[k]
        own = block(i, second)
        relay(own, (second_send.at[k, 0], second_recv.at[k, 0]), target(first, right))
        relay(own, (second_send.at[k, 1], second_recv.at[k, 1]), target(first, left))
        share(i, second, steps[k], 0)

    def begin():
        for other_z in range(4):
            for c in range(2):
                arrived(
                    kv.at[core, here, other_z // 2, pl.ds(c * 128 + (other_z % 2) * 64, 64)],
                    kv_recv.at[other_z, c],
                )
        own = block(first, second)
        for slot, i in enumerate((up, down, firsts[3])):
            relay(own, (first_send.at[slot], first_recv.at[slot]), target(i, second))
        spread(0)

    def first_hop(k):
        arrived(block(firsts[k], second), first_recv.at[k - 1])
        spread(k)

    def second_hop(k):
        i = firsts[k]
        arrived(block(i, left), second_recv.at[k, 0])
        relay(half(i, left, 0), (second_send.at[k, 2], second_recv.at[k, 2]), target(first, right))
        share(i, left, steps[k], -1)
        arrived(block(i, right), second_recv.at[k, 1])
        relay(half(i, right, 1), (second_send.at[k, 3], second_recv.at[k, 3]), target(first, left))
        share(i, right, steps[k], 1)

    def last_hop(k):
        i, j = firsts[k], wrap(second + 2)
        arrived(half(i, j, 0), second_recv.at[k, 2])
        arrived(half(i, j, 1), second_recv.at[k, 3])
        share(i, j, steps[k], 2)

    def queries_here():
        for role in range(2):
            for other_z in range(4):
                arrived(
                    landed.at[role, other_z // 2, pl.ds((other_z % 2) * 64, 64)],
                    qo_recv.at[role, other_z],
                )
        for s in range(2):
            for h in range(PER_GROUP):
                lanes, lines = pl.ds(h * 128, 128), pl.ds(h * CHUNK, CHUNK)
                qs[s, lines, :] = landed[0, s, :, lanes]
                os[s, lines, :] = landed[1, s, :, lanes]

    gather_events = {
        0: (begin, queries_here),
        1: (lambda: first_hop(1), lambda: first_hop(2), lambda: second_hop(0)),
        3: (lambda: first_hop(3),),
        5: (lambda: second_hop(1),),
        6: (lambda: second_hop(2),),
        7: (lambda: last_hop(0),),
        8: (lambda: second_hop(3),),
        10: (lambda: last_hop(1),),
        11: (lambda: last_hop(2),),
        12: (lambda: last_hop(3),),
    }

    def run(events, n):
        for at, actions in events.items():

            @pl.when(n == at)
            def _():
                for action in actions:
                    action()

    def block_of(code_x, code_y):
        return lax.rem(x + lax.rem(code_x, 4), 4) * 4 + lax.rem(y + lax.rem(code_y, 4), 4)

    def over_blocks(order, step):
        (start_x, more_x), (start_y, more_y) = codes(order, 0), codes(order, 1)

        def turn(n, carried):
            code_x, code_y = carried
            step(n, block_of(code_x, code_y))
            middle = lax.div(n + 1, 8) - lax.div(n + 1, 9)
            return lax.div(code_x, 4) + middle * more_x, lax.div(code_y, 4) + middle * more_y

        lax.fori_loop(0, 16, turn, (start_x + 0 * x, start_y + 0 * x))

    def items_of(b):
        return 1 + at_most(b, my_block) + at_most(b, 15 - my_block)

    def item(b, r):
        is_a = lax.rem(r, 2) * at_most(b, my_block)
        late = lax.div(r + 1, 2) - is_a
        return 1 - is_a, late, b + 16 * is_a + late * (32 - 2 * b)

    scale = FACTOR * math.log2(math.e)
    top[...] = jnp.full(top.shape, HIDDEN, F32)
    total[...] = jnp.zeros_like(total)
    dot[...] = jnp.zeros_like(dot)
    dq_acc[...] = jnp.zeros_like(dq_acc)

    def stats_step(n, b):
        run(gather_events, n)
        arrived(kv.at[1 - core, b], twin_recv.at[n])

        def stats(r, _):
            s, late, number = item(b, r)
            tile = late * 16 + b
            chunk = my_part + s * (63 - 2 * my_part)
            query_pos = chunk * CHUNK + lax.broadcasted_iota(jnp.int32, (1, CHUNK), 1)
            query_turn = turn_ref[pl.ds(chunk, 1), :]
            key_turn = jnp.concatenate(
                [
                    jnp.broadcast_to(turn_ref[pl.ds(2 * tile + i, 1), :], (128, 128)).T
                    for i in range(2)
                ],
                axis=0,
            )
            key_pos = tile * TILE + lax.broadcasted_iota(jnp.int32, (TILE, CHUNK), 0)
            visible = (key_pos <= query_pos) & (
                (key_turn == query_turn) | ((key_turn & 1) == 0)
            )
            logits = lax.dot_general(
                kv[0, b, late], qs[s], (((1,), (1,)), ((), ())), preferred_element_type=F32
            )
            bias = jnp.where(visible, 0.0, HIDDEN)
            logits = logits * scale + jnp.concatenate([bias] * PER_GROUP, axis=1)
            old_top = top[s]
            new_top = jnp.maximum(old_top, jnp.max(logits, axis=0, keepdims=True))
            shrink = jnp.exp2(old_top - new_top)
            weight = jnp.exp2(logits - new_top)
            grads = lax.dot_general(
                kv[1, b, late], os[s], (((1,), (1,)), ((), ())), preferred_element_type=F32
            )
            weights[number] = weight.astype(BF16)
            probs_grad[number] = grads.astype(BF16)
            tile_max[number] = new_top
            top[s] = new_top
            total[s] = total[s] * shrink + jnp.sum(weight, axis=0, keepdims=True)
            dot[s] = dot[s] * shrink + jnp.sum(weight * grads, axis=0, keepdims=True)
            return 0

        lax.fori_loop(0, items_of(b), stats, 0)

    over_blocks(NEAR_FIRST, stats_step)
    for s in range(2):
        inverse = 1.0 / total[s]
        total[s] = inverse
        dot[s] = dot[s] * inverse

    across = (wrap(second + 2), right, left, second)
    jumps = (2, 1, -1, 0)

    def chip_sum(a, b):
        i, j = firsts[a], across[b]
        at = index(i, j)
        arrived(twin.at[at], back_recv.at[slot_of(far, steps[a], jumps[b])])
        return partial[core, at].astype(F32) + twin[at].astype(F32)

    def ring_one(a):
        sums[a, 0] = chip_sum(a, 0).astype(BF16)
        for h, to in ((0, right), (1, left)):
            go(sums.at[a, 0, h], one.at[a, h], ring_send.at[a, h], ring_recv.at[a, h], target(first, to))

    def ring_two(a):
        for b, to in ((1, right), (2, left)):
            h = b - 1
            value = chip_sum(a, b)
            arrived(one.at[a, h], ring_recv.at[a, h])
            sums[a, b, 1 - h] = value[1 - h].astype(BF16)
            sums[a, b, h] = (value[h] + one[a, h].astype(F32)).astype(BF16)
            go(sums.at[a, b], two.at[a, h], ring_send.at[a, 2 + h], ring_recv.at[a, 2 + h], target(first, to))

    def home(a):
        value = chip_sum(a, 3)
        arrived(two.at[a, 0], ring_recv.at[a, 2])
        arrived(two.at[a, 1], ring_recv.at[a, 3])
        value = value + two[a, 0].astype(F32) + two[a, 1].astype(F32)
        line[a] = value.astype(BF16)
        i = firsts[a]
        bx, by = i + core * (second - i), second + core * (i - second)
        for other_z in range(4):
            for c in range(2):
                src = line.at[a, other_z // 2, pl.ds(c * 128 + (other_z % 2) * 64, 64)]
                dst = last.at[core, a, :, pl.ds(pl.multiple_of(z * 128, 128), 128)]
                args = (src, dst, last_send.at[a, other_z, c], last_recv.at[core, a, z])
                to = device(bx, by, other_z, c)
                if a:
                    go(*args, to)
                else:
                    go_or_keep((z == other_z) & (core == c), *args, to)

    reduce_events = {
        1: (lambda: ring_one(3),),
        4: (lambda: ring_one(2),),
        5: (lambda: ring_one(1),),
        6: (lambda: ring_two(3),),
        7: (lambda: ring_one(0),),
        12: (lambda: ring_two(0), lambda: home(3)),
        14: (lambda: ring_two(2),),
        15: (lambda: ring_two(1),),
    }

    def backward_step(n, b):
        def terms(r, _):
            s, late, number = item(b, r)
            by = jnp.exp2(tile_max[number] - top[s]) * total[s]
            attention = weights[number].astype(F32) * by
            logit_grad = (attention * (probs_grad[number].astype(F32) - dot[s])).astype(BF16)
            key_term = jnp.dot(logit_grad, qs[s], preferred_element_type=F32) * FACTOR
            value_term = jnp.dot(attention.astype(BF16), os[s], preferred_element_type=F32)
            dq_acc[s] += lax.dot_general(
                logit_grad, kv[0, b, late], (((0,), (0,)), ((), ())), preferred_element_type=F32
            )
            key_term += jnp.where(s == 0, term[0], 0.0)
            value_term += jnp.where(s == 0, term[1], 0.0)
            term[0] = key_term
            term[1] = value_term
            partial[0, b, late] = key_term.astype(BF16)
            partial[1, b, late] = value_term.astype(BF16)
            return 0

        lax.fori_loop(0, items_of(b), terms, 0)

        @pl.when(b > 15 - my_block)
        def _():
            partial[0, b, 1] = jnp.zeros((TILE, HEAD_SIZE), BF16)
            partial[1, b, 1] = jnp.zeros((TILE, HEAD_SIZE), BF16)

        send(partial.at[1 - core, b], twin.at[b], back_send.at[n], back_recv.at[n], other_core).start()
        run(reduce_events, n)

    term[...] = jnp.zeros_like(term)
    over_blocks(FAR_FIRST, backward_step)

    for s in range(2):
        for h in range(PER_GROUP):
            dq_own[s, :, pl.ds(h * 128, 128)] = (
                dq_acc[s, pl.ds(h * CHUNK, CHUNK), :] * FACTOR
            ).astype(BF16)
    for other_z in range(4):
        s = other_z // 2
        flip = lax.rem(s + odd, 2)
        to = device(x + flip * (3 - 2 * x), y + flip * (3 - 2 * y), other_z, core + flip * (1 - 2 * core))
        go_or_keep(
            (flip == 0) & (z == other_z),
            dq_own.at[s, pl.ds((other_z % 2) * 64, 64)],
            dq_out.at[:, pl.ds(pl.multiple_of(z * 512, 512), 512)],
            dq_send.at[other_z], dq_recv.at[z], to,
        )
    home(2)
    home(1)
    home(0)

    for role, out in ((0, dk_out), (1, dv_out)):
        value = None
        for a in range(4):
            for other_z in range(4):
                arrived(last.at[role, a, :, pl.ds(other_z * 128, 128)], last_recv.at[role, a, other_z])
            share_in = last[role, a].astype(F32)
            value = share_in if value is None else value + share_in
        out[...] = value.astype(BF16)
    for other_z in range(4):
        arrived(dq_out.at[:, pl.ds(other_z * 512, 512)], dq_recv.at[other_z])

    whole, halved, piece = kv.at[0, 0], kv.at[0, 0, 0], line.at[0, 0, pl.ds(0, 64)]
    for r in range(1, 4):
        for role in range(2):
            arrived(k_ref.at[:, pl.ds(0, 128)], kv_send.at[role, r])
            arrived(q_ref.at[:, pl.ds(0, 512)], qo_send.at[role, r])
        arrived(whole, first_send.at[r - 1])
        for other_z in range(4):
            for c in range(2):
                arrived(piece, last_send.at[r, other_z, c])
    for k in range(4):
        for h in range(2):
            arrived(whole, second_send.at[k, h])
            arrived(halved, second_send.at[k, 2 + h])
            arrived(halved, ring_send.at[k, h])
            arrived(whole, ring_send.at[k, 2 + h])
    for n in range(16):
        arrived(whole, twin_send.at[n])
        arrived(whole, back_send.at[n])

    @pl.when(core == 0)
    def _():
        arrived(v_ref.at[:, pl.ds(0, 128)], kv_send.at[1, 0])

    @pl.when(core == 1)
    def _():
        arrived(k_ref.at[:, pl.ds(0, 128)], kv_send.at[0, 0])

    @pl.when(lax.rem(z_hi + z_lo, 2) == 1)
    def _():
        for role in range(2):
            arrived(q_ref.at[:, pl.ds(0, 512)], qo_send.at[role, 0])

    for other_z in range(4):
        for c in range(2):

            @pl.when(jnp.logical_not((z == other_z) & (core == c)))
            def _():
                arrived(piece, last_send.at[0, other_z, c])

        flip = lax.rem(other_z // 2 + odd, 2)

        @pl.when(jnp.logical_not((flip == 0) & (z == other_z)))
        def _():
            arrived(dq_own.at[0, pl.ds(0, 64)], dq_send.at[other_z])


ANY = pl.BlockSpec(memory_space=pl.ANY)
VMEM = pl.BlockSpec(memory_space=pltpu.VMEM)
DMA = pltpu.SemaphoreType.DMA


def body(queries, keys, values, grad_out, turn_ids):
    block = (2, TILE, HEAD_SIZE)
    return pl.pallas_call(
        kernel,
        out_shape=(
            jax.ShapeDtypeStruct((64, 2048), BF16),
            jax.ShapeDtypeStruct((64, 512), BF16),
            jax.ShapeDtypeStruct((64, 512), BF16),
        ),
        in_specs=[VMEM] + [ANY] * 4,
        out_specs=(ANY, VMEM, VMEM),
        scratch_shapes=[
            pltpu.VMEM((2, 16) + block, BF16),
            pltpu.VMEM((2, 2, CHUNK, 512), BF16),
            pltpu.VMEM((2, ROWS, HEAD_SIZE), BF16),
            pltpu.VMEM((2, ROWS, HEAD_SIZE), BF16),
            pltpu.VMEM((ITEMS, TILE, ROWS), BF16),
            pltpu.VMEM((ITEMS, TILE, ROWS), BF16),
            pltpu.VMEM((ITEMS, 1, ROWS), F32),
            pltpu.VMEM((2, 1, ROWS), F32),
            pltpu.VMEM((2, 1, ROWS), F32),
            pltpu.VMEM((2, 1, ROWS), F32),
            pltpu.VMEM((2, ROWS, HEAD_SIZE), F32),
            pltpu.VMEM((2, CHUNK, 512), BF16),
            pltpu.VMEM((2, TILE, HEAD_SIZE), F32),
            pltpu.VMEM((2, 16) + block, BF16),
            pltpu.VMEM((16,) + block, BF16),
            pltpu.VMEM((4, 3) + block, BF16),
            pltpu.VMEM((4, 2, TILE, HEAD_SIZE), BF16),
            pltpu.VMEM((4, 2) + block, BF16),
            pltpu.VMEM((4,) + block, BF16),
            pltpu.VMEM((2, 4, 64, 512), BF16),
            DMA((2, 4)), DMA((4, 2)),
            DMA((2, 4)), DMA((2, 4)),
            DMA((3,)), DMA((3,)),
            DMA((4, 4)), DMA((4, 4)),
            DMA((16,)), DMA((16,)),
            DMA((16,)), DMA((16,)),
            DMA((4, 4)), DMA((4, 4)),
            DMA((4, 4, 2)), DMA((2, 4, 4)),
            DMA((4,)), DMA((4,)),
        ],
        compiler_params=pltpu.CompilerParams(
            collective_id=0, has_side_effects=True, vmem_limit_bytes=58 << 20
        ),
        name="attention_backward",
    )(turn_ids.reshape(64, CHUNK), queries, keys, values, grad_out)


def solution(mesh):
    spread = P(("blk", "head"), None)
    return jax.shard_map(
        body,
        mesh=mesh,
        in_specs=(spread,) * 4 + (P(),),
        out_specs=(spread,) * 3,
        check_vma=False,
    )
```

time: 1030 us -> 77.2 us (0.07)
  waiting for transfers between devices: 749 us -> 0 us
  matrix products: 87.5 us -> 0 us
  local copies, waits for them, and re-layouts: 82.1 us -> 3.2 us
  Pallas kernels: 0 us -> 73.1 us
  other arithmetic: 60.5 us -> 0 us
  starting transfers between devices: 20.4 us -> 0 us
  between operations: 13.9 us -> 0.65 us
    reduce_scatter x2 -> x0, waiting for transfers between devices: 668 us -> none  [the longest x1 338 us: body(): lax.psum_scatter(grad_values_all, 'blk', scatter_dimension=0, tiled=True)]
    dot_general x112 -> x0, matrix products: 87.5 us -> none  [the longest x16 19.8 us: backward_step(): jnp.einsum('grtb,tgrd->bgd', rounded, grad_four, preferred_element_type=j...]
    pallas_call x0 -> x1, Pallas kernels: none -> 73.1 us  [body(): pl.pallas_call(kernel, out_shape=(jax.ShapeDtypeStruct((64, 2048), BF16),...]
    all_gather x2 -> x0, waiting for transfers between devices: 71.4 us -> none  [the longest x1 53.8 us: body(): lax.all_gather(key_here, 'blk', axis=0, tiled=True)]
    dynamic_slice x49 -> x0, local copies, waits for them, and re-layouts: 50.7 us -> none  [the longest x32 32.8 us: key_slab(): lax.dynamic_slice_in_dim(whole_keys, begin_row, block_size, 0)]
    eq x48 -> x0, other arithmetic: 37.1 us -> none  [visible_mask(): kept_turn = (key_turn % 2 == 0)[None, :]]
    all_to_all x6 -> x0, starting transfers between devices: 20.2 us -> none  [the longest x1 3.44 us: body(): lax.all_to_all(queries, 'head', split_axis=1, concat_axis=0, tiled=True)]
    and x48 -> x0, other arithmetic: 13 us -> none  [visible_mask(): return causal & (same_turn | kept_turn)]
  transfers between devices with their start and end apart: 10 -> 0, of which waited for: 8 -> 0; matrix products, arithmetic and copies ran while one was open for 6% -> 0% of each run, Pallas kernels for 0% -> 0%
where the time goes in v2:
time: 77.2 us; the launch traced here: 77 us
  Pallas kernels  73.1 us (95%)
  local copies, waits for them, and re-layouts  3.2 us (4%)
    pallas_call x1, Pallas kernels, body(): pl.pallas_call(kernel, out_shape=(jax.ShapeDtypeStruct((64, 2048), BF16),...  73.1 us
    unnamed x7, local copies, waits for them, and re-layouts  3.2 us

profile of v2, /device:TPU:1, one launch (start us, length us, event | category | flops | bytes accessed | tf_op | source)
XLA Modules:
  0.0 77.0 jit_solution(8524483566283067705)
XLA Ops:
  0.6 73.1 %attention_backward.1 = (bf16[64,2048]{1,0:T(8,128)(2,1)}, bf16[64,512]{1,0:T(8,128)(2,1)}, bf16[64,512]{1,0:T(8,128)(2,1)}) custom-call(s32[64,128]{1,0:T(8,128)} %bitcast.1, bf16[64,2048]{1,0:T(8,128)(2,1)} %q_ref.1, bf16[64,512]{1,0:T(8,128)(2,1)} %k_ref.1, bf16[64,512]{1,0:T(8,128)(2,1)} %v_ref.1, bf16[64,2048]{1,0:T(8,128)(2,1)} %o_ref.1), custom_call_target="tpu_custom_call" | custom-call | tf_op jit(solution)/shard_map/attention_backward/pallas_call | solution.py:492
  73.8 0.0 copy-start.1
  73.8 1.7 %copy.11 = bf16[64,2048]{1,0:T(8,128)(2,1)} copy(bf16[64,2048]{1,0:T(8,128)(2,1)} %get-tuple-element.6) | data formatting | bytes 524288
  75.5 0.0 copy-done.1
  75.5 0.0 copy-start
  75.5 0.6 copy.12
  76.1 0.2 copy-done
  76.3 0.6 copy.13
Async XLA Ops:
  73.8 1.7 %copy-start.1 = (bf16[64,512]{1,0:T(8,128)(2,1)S(1)}, bf16[64,512]{1,0:T(8,128)(2,1)}, u32[]{:S(2)}) copy-start(bf16[64,512]{1,0:T(8,128)(2,1)} %get-tuple-element.7) | copy-start | bytes 196612
  75.5 0.9 %copy-start = (bf16[64,512]{1,0:T(8,128)(2,1)S(1)}, bf16[64,512]{1,0:T(8,128)(2,1)}, u32[]{:S(2)}) copy-start(bf16[64,512]{1,0:T(8,128)(2,1)} %get-tuple-element.8) | copy-start | bytes 196612

commit v3 on v2

--- a/solution.py
+++ b/solution.py
@@ -58,13 +58,11 @@
         other_z = lax.rem(z + r, 4)
         if r:
             others.append(device(x, y, other_z, core))
+            others.append(device(wrap(x + r * (1 - core)), wrap(y + r * core), z, core))
         others.append(device(x, y, other_z, 1 - core))
         others.append(device(3 - x, 3 - y, other_z, 1 - core))
-        for step in (1, 2, 3):
-            others.append(device(wrap(x + step), y, other_z, 0))
-            others.append(device(wrap(x + step), y, other_z, 1))
-            others.append(device(x, wrap(y + step), other_z, 0))
-            others.append(device(x, wrap(y + step), other_z, 1))
+    for step in (-1, 1):
+        others.append(device(wrap(x + step * core), wrap(y + step * (1 - core)), z, core))
     barrier = pltpu.get_barrier_semaphore()
     for other in others:
         pl.semaphore_signal(barrier, inc=1, device_id=other, device_id_type=MESH)
@@ -81,9 +79,9 @@
 
 
 def kernel(
-    turn_ref, q_ref, k_ref, v_ref, o_ref, dq_out, dk_out, dv_out,
+    turn_ref, q_ref, k_ref, v_ref, o_ref, dq_out, last,
     kv, landed, qs, os, weights, probs_grad, tile_max, top, total, dot, dq_acc, dq_own,
-    term, partial, twin, sums, one, two, line, last,
+    term, partial, twin, sums, one, two, line,
     kv_send, kv_recv, qo_send, qo_recv, first_send, first_recv, second_send, second_recv,
     twin_send, twin_recv, back_send, back_recv, ring_send, ring_recv, last_send, last_recv,
     dq_send, dq_recv,
@@ -425,14 +423,10 @@
     home(1)
     home(0)
 
-    for role, out in ((0, dk_out), (1, dv_out)):
-        value = None
+    for role in range(2):
         for a in range(4):
             for other_z in range(4):
                 arrived(last.at[role, a, :, pl.ds(other_z * 128, 128)], last_recv.at[role, a, other_z])
-            share_in = last[role, a].astype(F32)
-            value = share_in if value is None else value + share_in
-        out[...] = value.astype(BF16)
     for other_z in range(4):
         arrived(dq_out.at[:, pl.ds(other_z * 512, 512)], dq_recv.at[other_z])
 
@@ -482,6 +476,15 @@
             arrived(dq_own.at[0, pl.ds(0, 64)], dq_send.at[other_z])
 
 
+def finish_kernel(dq_ref, dkv_ref, dq_out, dk_out, dv_out):
+    dq_out[...] = dq_ref[...]
+    for role, out in ((0, dk_out), (1, dv_out)):
+        value = dkv_ref[role, 0].astype(F32)
+        for a in range(1, 4):
+            value = value + dkv_ref[role, a].astype(F32)
+        out[...] = value.astype(BF16)
+
+
 ANY = pl.BlockSpec(memory_space=pl.ANY)
 VMEM = pl.BlockSpec(memory_space=pltpu.VMEM)
 DMA = pltpu.SemaphoreType.DMA
@@ -489,15 +492,14 @@
 
 def body(queries, keys, values, grad_out, turn_ids):
     block = (2, TILE, HEAD_SIZE)
-    return pl.pallas_call(
+    dq, dkv = pl.pallas_call(
         kernel,
         out_shape=(
             jax.ShapeDtypeStruct((64, 2048), BF16),
-            jax.ShapeDtypeStruct((64, 512), BF16),
-            jax.ShapeDtypeStruct((64, 512), BF16),
+            jax.ShapeDtypeStruct((2, 4, 64, 512), BF16),
         ),
         in_specs=[VMEM] + [ANY] * 4,
-        out_specs=(ANY, VMEM, VMEM),
+        out_specs=(ANY, ANY),
         scratch_shapes=[
             pltpu.VMEM((2, 16) + block, BF16),
             pltpu.VMEM((2, 2, CHUNK, 512), BF16),
@@ -518,7 +520,6 @@
             pltpu.VMEM((4, 2, TILE, HEAD_SIZE), BF16),
             pltpu.VMEM((4, 2) + block, BF16),
             pltpu.VMEM((4,) + block, BF16),
-            pltpu.VMEM((2, 4, 64, 512), BF16),
             DMA((2, 4)), DMA((4, 2)),
             DMA((2, 4)), DMA((2, 4)),
             DMA((3,)), DMA((3,)),
@@ -534,6 +535,18 @@
         ),
         name="attention_backward",
     )(turn_ids.reshape(64, CHUNK), queries, keys, values, grad_out)
+    return pl.pallas_call(
+        finish_kernel,
+        out_shape=(
+            jax.ShapeDtypeStruct((64, 2048), BF16),
+            jax.ShapeDtypeStruct((64, 512), BF16),
+            jax.ShapeDtypeStruct((64, 512), BF16),
+        ),
+        in_specs=[VMEM] * 2,
+        out_specs=(VMEM,) * 3,
+        compiler_params=pltpu.CompilerParams(vmem_limit_bytes=60 << 20),
+        name="finish",
+    )(dq, dkv)
 
 
 def solution(mesh):

time: 77.2 us -> 74.8 us (0.969)
  local copies, waits for them, and re-layouts: 3.2 us -> 0 us
  Pallas kernels: 73.1 us -> 73.9 us
    unnamed x7 -> x0, local copies, waits for them, and re-layouts: 3.2 us -> none
    pallas_call x0 -> x1, Pallas kernels: none -> 1.89 us  [body(): pl.pallas_call(finish_kernel, out_shape=(jax.ShapeDtypeStruct((64, 2048),...]
    pallas_call x1, Pallas kernels: 73.1 us -> 72 us  [body(): pl.pallas_call(kernel, out_shape=(jax.ShapeDtypeStruct((64, 2048), BF16),...]
where the time goes in v3:
time: 74.8 us; the launch traced here: 74.6 us
  Pallas kernels  73.9 us (99%)
    pallas_call x1, Pallas kernels, body(): pl.pallas_call(kernel, out_shape=(jax.ShapeDtypeStruct((64, 2048), BF16),...  72 us
    pallas_call x1, Pallas kernels, body(): pl.pallas_call(finish_kernel, out_shape=(jax.ShapeDtypeStruct((64, 2048),...  1.89 us

profile of v3, /device:TPU:1, one launch (start us, length us, event | category | flops | bytes accessed | tf_op | source)
XLA Modules:
  0.0 74.6 jit_solution(7381268520094503239)
XLA Ops:
  0.6 72.0 %attention_backward.1 = (bf16[64,2048]{1,0:T(8,128)(2,1)}, bf16[2,4,64,512]{3,2,1,0:T(8,128)(2,1)}) custom-call(s32[64,128]{1,0:T(8,128)} %bitcast.1, bf16[64,2048]{1,0:T(8,128)(2,1)} %q_ref.1, bf16[64,512]{1,0:T(8,128)(2,1)} %k_ref.1, bf16[64,512]{1,0:T(8,128)(2,1)} %v_ref.1, bf16[64,2048]{1,0:T(8,128)(2,1)} %o_ref.1), custom_call_target="tpu_custom_call" | custom-call | tf_op jit(solution)/shard_map/attention_backward/pallas_call | solution.py:495
  72.7 1.9 %finish.1 = (bf16[64,2048]{1,0:T(8,128)(2,1)}, bf16[64,512]{1,0:T(8,128)(2,1)}, bf16[64,512]{1,0:T(8,128)(2,1)}) custom-call(bf16[64,2048]{1,0:T(8,128)(2,1)} %get-tuple-element.5.dq_ref, bf16[2,4,64,512]{3,2,1,0:T(8,128)(2,1)} %get-tuple-element.6.dkv_ref), custom_call_target="tpu_custom_call" | custom-call | tf_op jit(solution)/shard_map/finish/pallas_call | solution.py:538

commit v4 on v3

--- a/solution.py
+++ b/solution.py
@@ -58,11 +58,11 @@
         other_z = lax.rem(z + r, 4)
         if r:
             others.append(device(x, y, other_z, core))
-            others.append(device(wrap(x + r * (1 - core)), wrap(y + r * core), z, core))
         others.append(device(x, y, other_z, 1 - core))
         others.append(device(3 - x, 3 - y, other_z, 1 - core))
     for step in (-1, 1):
-        others.append(device(wrap(x + step * core), wrap(y + step * (1 - core)), z, core))
+        others.append(device(wrap(x + step), y, z, core))
+        others.append(device(x, wrap(y + step), z, core))
     barrier = pltpu.get_barrier_semaphore()
     for other in others:
         pl.semaphore_signal(barrier, inc=1, device_id=other, device_id_type=MESH)
@@ -81,10 +81,10 @@
 def kernel(
     turn_ref, q_ref, k_ref, v_ref, o_ref, dq_out, last,
     kv, landed, qs, os, weights, probs_grad, tile_max, top, total, dot, dq_acc, dq_own,
-    term, partial, twin, sums, one, two, line,
+    partial, twin, sums, one, two, line, line_in,
     kv_send, kv_recv, qo_send, qo_recv, first_send, first_recv, second_send, second_recv,
     twin_send, twin_recv, back_send, back_recv, ring_send, ring_recv, last_send, last_recv,
-    dq_send, dq_recv,
+    line_send, line_recv,     dq_send, dq_recv,
 ):
     blk = lax.axis_index("blk")
     z_lo = lax.axis_index("head")
@@ -185,12 +185,18 @@
                     kv_recv.at[other_z, c],
                 )
         own = block(first, second)
-        for slot, i in enumerate((up, down, firsts[3])):
-            relay(own, (first_send.at[slot], first_recv.at[slot]), target(i, second))
+        relay(own, (first_send.at[0], first_recv.at[0]), target(up, second))
+        relay(own, (first_send.at[1], first_recv.at[1]), target(down, second))
         spread(0)
 
     def first_hop(k):
-        arrived(block(firsts[k], second), first_recv.at[k - 1])
+        if k < 3:
+            h, to = k - 1, (up, down)[k - 1]
+            arrived(block(firsts[k], second), first_recv.at[h])
+            relay(half(firsts[k], second, h), (first_send.at[2 + h], first_recv.at[2 + h]), target(to, second))
+        else:
+            for h in range(2):
+                arrived(half(firsts[k], second, h), first_recv.at[2 + h])
         spread(k)
 
     def second_hop(k):
@@ -256,13 +262,19 @@
 
         lax.fori_loop(0, 16, turn, (start_x + 0 * x, start_y + 0 * x))
 
-    def items_of(b):
-        return 1 + at_most(b, my_block) + at_most(b, 15 - my_block)
-
-    def item(b, r):
-        is_a = lax.rem(r, 2) * at_most(b, my_block)
-        late = lax.div(r + 1, 2) - is_a
-        return 1 - is_a, late, b + 16 * is_a + late * (32 - 2 * b)
+    def in_full(b, work):
+        kind = at_most(b, my_block) + 2 * at_most(b, 15 - my_block)
+        for number in range(4):
+
+            @pl.when(kind == number)
+            def _():
+                work(number % 2, number // 2)
+
+    def tiles_of(s, with_late):
+        return (0, 1) if s and with_late else (0,)
+
+    def number_of(b, s, late):
+        return (32 - b) if late else b + 16 * (1 - s)
 
     scale = FACTOR * math.log2(math.e)
     top[...] = jnp.full(top.shape, HIDDEN, F32)
@@ -274,44 +286,57 @@
         run(gather_events, n)
         arrived(kv.at[1 - core, b], twin_recv.at[n])
 
-        def stats(r, _):
-            s, late, number = item(b, r)
-            tile = late * 16 + b
-            chunk = my_part + s * (63 - 2 * my_part)
-            query_pos = chunk * CHUNK + lax.broadcasted_iota(jnp.int32, (1, CHUNK), 1)
-            query_turn = turn_ref[pl.ds(chunk, 1), :]
-            key_turn = jnp.concatenate(
-                [
-                    jnp.broadcast_to(turn_ref[pl.ds(2 * tile + i, 1), :], (128, 128)).T
-                    for i in range(2)
-                ],
-                axis=0,
-            )
-            key_pos = tile * TILE + lax.broadcasted_iota(jnp.int32, (TILE, CHUNK), 0)
-            visible = (key_pos <= query_pos) & (
-                (key_turn == query_turn) | ((key_turn & 1) == 0)
-            )
-            logits = lax.dot_general(
-                kv[0, b, late], qs[s], (((1,), (1,)), ((), ())), preferred_element_type=F32
-            )
-            bias = jnp.where(visible, 0.0, HIDDEN)
-            logits = logits * scale + jnp.concatenate([bias] * PER_GROUP, axis=1)
-            old_top = top[s]
-            new_top = jnp.maximum(old_top, jnp.max(logits, axis=0, keepdims=True))
-            shrink = jnp.exp2(old_top - new_top)
-            weight = jnp.exp2(logits - new_top)
-            grads = lax.dot_general(
-                kv[1, b, late], os[s], (((1,), (1,)), ((), ())), preferred_element_type=F32
-            )
-            weights[number] = weight.astype(BF16)
-            probs_grad[number] = grads.astype(BF16)
-            tile_max[number] = new_top
-            top[s] = new_top
-            total[s] = total[s] * shrink + jnp.sum(weight, axis=0, keepdims=True)
-            dot[s] = dot[s] * shrink + jnp.sum(weight * grads, axis=0, keepdims=True)
-            return 0
-
-        lax.fori_loop(0, items_of(b), stats, 0)
+        def stats(with_a, with_late):
+            key_turns = [
+                jnp.concatenate(
+                    [
+                        jnp.broadcast_to(turn_ref[pl.ds(2 * (late * 16 + b) + i, 1), :], (128, 128)).T
+                        for i in range(2)
+                    ],
+                    axis=0,
+                )
+                for late in range(1 + with_late)
+            ]
+            for s in (1, 0) if with_a else (1,):
+                chunk = my_part if s == 0 else 63 - my_part
+                query_pos = chunk * CHUNK + lax.broadcasted_iota(jnp.int32, (1, CHUNK), 1)
+                query_turn = turn_ref[pl.ds(chunk, 1), :]
+                old_top = top[s]
+                new_top = old_top
+                parts = []
+                for late in tiles_of(s, with_late):
+                    key_turn = key_turns[late]
+                    key_pos = (late * 16 + b) * TILE + lax.broadcasted_iota(
+                        jnp.int32, (TILE, CHUNK), 0
+                    )
+                    visible = (key_pos <= query_pos) & (
+                        (key_turn == query_turn) | ((key_turn & 1) == 0)
+                    )
+                    logits = lax.dot_general(
+                        kv[0, b, late], qs[s], (((1,), (1,)), ((), ())), preferred_element_type=F32
+                    )
+                    bias = jnp.where(visible, 0.0, HIDDEN)
+                    logits = logits * scale + jnp.concatenate([bias] * PER_GROUP, axis=1)
+                    new_top = jnp.maximum(new_top, jnp.max(logits, axis=0, keepdims=True))
+                    grads = lax.dot_general(
+                        kv[1, b, late], os[s], (((1,), (1,)), ((), ())), preferred_element_type=F32
+                    )
+                    parts.append((late, logits, grads))
+                shrink = jnp.exp2(old_top - new_top)
+                new_total, new_dot = total[s] * shrink, dot[s] * shrink
+                for late, logits, grads in parts:
+                    number = number_of(b, s, late)
+                    weight = jnp.exp2(logits - new_top)
+                    weights[number] = weight.astype(BF16)
+                    probs_grad[number] = grads.astype(BF16)
+                    tile_max[number] = new_top
+                    new_total += jnp.sum(weight, axis=0, keepdims=True)
+                    new_dot += jnp.sum(weight * grads, axis=0, keepdims=True)
+                top[s] = new_top
+                total[s] = new_total
+                dot[s] = new_dot
+
+        in_full(b, stats)
 
     over_blocks(NEAR_FIRST, stats_step)
     for s in range(2):
@@ -347,7 +372,18 @@
         arrived(two.at[a, 0], ring_recv.at[a, 2])
         arrived(two.at[a, 1], ring_recv.at[a, 3])
         value = value + two[a, 0].astype(F32) + two[a, 1].astype(F32)
-        line[a] = value.astype(BF16)
+        if a == 3:
+            line[a] = value.astype(BF16)
+            for h, to in ((0, up), (1, down)):
+                go(line.at[a, h], line_in.at[h], line_send.at[h], line_recv.at[h], target(to, second))
+            return
+        if a:
+            h = 2 - a
+            arrived(line_in.at[h], line_recv.at[h])
+            line[a, 1 - h] = value[1 - h].astype(BF16)
+            line[a, h] = (value[h] + line_in[h].astype(F32)).astype(BF16)
+        else:
+            line[a] = value.astype(BF16)
         i = firsts[a]
         bx, by = i + core * (second - i), second + core * (i - second)
         for other_z in range(4):
@@ -367,43 +403,45 @@
         5: (lambda: ring_one(1),),
         6: (lambda: ring_two(3),),
         7: (lambda: ring_one(0),),
-        12: (lambda: ring_two(0), lambda: home(3)),
+        11: (lambda: ring_two(0), lambda: home(3)),
         14: (lambda: ring_two(2),),
         15: (lambda: ring_two(1),),
     }
 
     def backward_step(n, b):
-        def terms(r, _):
-            s, late, number = item(b, r)
-            by = jnp.exp2(tile_max[number] - top[s]) * total[s]
-            attention = weights[number].astype(F32) * by
-            logit_grad = (attention * (probs_grad[number].astype(F32) - dot[s])).astype(BF16)
-            key_term = jnp.dot(logit_grad, qs[s], preferred_element_type=F32) * FACTOR
-            value_term = jnp.dot(attention.astype(BF16), os[s], preferred_element_type=F32)
-            dq_acc[s] += lax.dot_general(
-                logit_grad, kv[0, b, late], (((0,), (0,)), ((), ())), preferred_element_type=F32
-            )
-            key_term += jnp.where(s == 0, term[0], 0.0)
-            value_term += jnp.where(s == 0, term[1], 0.0)
-            term[0] = key_term
-            term[1] = value_term
-            partial[0, b, late] = key_term.astype(BF16)
-            partial[1, b, late] = value_term.astype(BF16)
-            return 0
-
-        lax.fori_loop(0, items_of(b), terms, 0)
-
-        @pl.when(b > 15 - my_block)
-        def _():
-            partial[0, b, 1] = jnp.zeros((TILE, HEAD_SIZE), BF16)
-            partial[1, b, 1] = jnp.zeros((TILE, HEAD_SIZE), BF16)
-
+        def terms(with_a, with_late):
+            keys_sum, values_sum = [0.0, 0.0], [0.0, 0.0]
+            for s in (1, 0) if with_a else (1,):
+                query_sum = dq_acc[s]
+                for late in tiles_of(s, with_late):
+                    number = number_of(b, s, late)
+                    by = jnp.exp2(tile_max[number] - top[s]) * total[s]
+                    attention = weights[number].astype(F32) * by
+                    logit_grad = (attention * (probs_grad[number].astype(F32) - dot[s])).astype(BF16)
+                    values_sum[late] += jnp.dot(
+                        attention.astype(BF16), os[s], preferred_element_type=F32
+                    )
+                    keys_sum[late] += jnp.dot(logit_grad, qs[s], preferred_element_type=F32)
+                    query_sum += lax.dot_general(
+                        logit_grad, kv[0, b, late], (((0,), (0,)), ((), ())),
+                        preferred_element_type=F32,
+                    )
+                dq_acc[s] = query_sum
+            for late in range(2):
+                if late <= with_late:
+                    partial[0, b, late] = (keys_sum[late] * FACTOR).astype(BF16)
+                    partial[1, b, late] = values_sum[late].astype(BF16)
+                else:
+                    partial[0, b, late] = jnp.zeros((TILE, HEAD_SIZE), BF16)
+                    partial[1, b, late] = jnp.zeros((TILE, HEAD_SIZE), BF16)
+
+        in_full(b, terms)
         send(partial.at[1 - core, b], twin.at[b], back_send.at[n], back_recv.at[n], other_core).start()
         run(reduce_events, n)
 
-    term[...] = jnp.zeros_like(term)
     over_blocks(FAR_FIRST, backward_step)
 
+    home(0)
     for s in range(2):
         for h in range(PER_GROUP):
             dq_own[s, :, pl.ds(h * 128, 128)] = (
@@ -421,10 +459,9 @@
         )
     home(2)
     home(1)
-    home(0)
 
     for role in range(2):
-        for a in range(4):
+        for a in range(3):
             for other_z in range(4):
                 arrived(last.at[role, a, :, pl.ds(other_z * 128, 128)], last_recv.at[role, a, other_z])
     for other_z in range(4):
@@ -435,10 +472,14 @@
         for role in range(2):
             arrived(k_ref.at[:, pl.ds(0, 128)], kv_send.at[role, r])
             arrived(q_ref.at[:, pl.ds(0, 512)], qo_send.at[role, r])
-        arrived(whole, first_send.at[r - 1])
+    for r in range(1, 3):
         for other_z in range(4):
             for c in range(2):
                 arrived(piece, last_send.at[r, other_z, c])
+    for h in range(2):
+        arrived(whole, first_send.at[h])
+        arrived(halved, first_send.at[2 + h])
+        arrived(halved, line_send.at[h])
     for k in range(4):
         for h in range(2):
             arrived(whole, second_send.at[k, h])
@@ -480,7 +521,7 @@
     dq_out[...] = dq_ref[...]
     for role, out in ((0, dk_out), (1, dv_out)):
         value = dkv_ref[role, 0].astype(F32)
-        for a in range(1, 4):
+        for a in range(1, 3):
             value = value + dkv_ref[role, a].astype(F32)
         out[...] = value.astype(BF16)
 
@@ -496,7 +537,7 @@
         kernel,
         out_shape=(
             jax.ShapeDtypeStruct((64, 2048), BF16),
-            jax.ShapeDtypeStruct((2, 4, 64, 512), BF16),
+            jax.ShapeDtypeStruct((2, 3, 64, 512), BF16),
         ),
         in_specs=[VMEM] + [ANY] * 4,
         out_specs=(ANY, ANY),
@@ -513,21 +554,22 @@
             pltpu.VMEM((2, 1, ROWS), F32),
             pltpu.VMEM((2, ROWS, HEAD_SIZE), F32),
             pltpu.VMEM((2, CHUNK, 512), BF16),
-            pltpu.VMEM((2, TILE, HEAD_SIZE), F32),
             pltpu.VMEM((2, 16) + block, BF16),
             pltpu.VMEM((16,) + block, BF16),
             pltpu.VMEM((4, 3) + block, BF16),
             pltpu.VMEM((4, 2, TILE, HEAD_SIZE), BF16),
             pltpu.VMEM((4, 2) + block, BF16),
             pltpu.VMEM((4,) + block, BF16),
+            pltpu.VMEM(block, BF16),
             DMA((2, 4)), DMA((4, 2)),
             DMA((2, 4)), DMA((2, 4)),
-            DMA((3,)), DMA((3,)),
+            DMA((4,)), DMA((4,)),
             DMA((4, 4)), DMA((4, 4)),
             DMA((16,)), DMA((16,)),
             DMA((16,)), DMA((16,)),
             DMA((4, 4)), DMA((4, 4)),
-            DMA((4, 4, 2)), DMA((2, 4, 4)),
+            DMA((3, 4, 2)), DMA((2, 3, 4)),
+            DMA((2,)), DMA((2,)),
             DMA((4,)), DMA((4,)),
         ],
         compiler_params=pltpu.CompilerParams(

time: 74.8 us -> 70.8 us (0.947)
  the two profiles are of different devices: /device:TPU:1 before, /device:TPU:3 now
where the time goes in v4:
time: 70.8 us; the launch traced here: 70.6 us
  Pallas kernels  70 us (99%)
    pallas_call x1, Pallas kernels, body(): pl.pallas_call(kernel, out_shape=(jax.ShapeDtypeStruct((64, 2048), BF16),...  68.1 us
    pallas_call x1, Pallas kernels, body(): pl.pallas_call(finish_kernel, out_shape=(jax.ShapeDtypeStruct((64, 2048),...  1.84 us

profile of v4, /device:TPU:3, one launch (start us, length us, event | category | flops | bytes accessed | tf_op | source)
XLA Modules:
  0.0 70.6 jit_solution(4719378645574936943)
XLA Ops:
  0.6 68.1 %attention_backward.1 = (bf16[64,2048]{1,0:T(8,128)(2,1)}, bf16[2,3,64,512]{3,2,1,0:T(8,128)(2,1)}) custom-call(s32[64,128]{1,0:T(8,128)} %bitcast.1, bf16[64,2048]{1,0:T(8,128)(2,1)} %q_ref.1, bf16[64,512]{1,0:T(8,128)(2,1)} %k_ref.1, bf16[64,512]{1,0:T(8,128)(2,1)} %v_ref.1, bf16[64,2048]{1,0:T(8,128)(2,1)} %o_ref.1), custom_call_target="tpu_custom_call" | custom-call | tf_op jit(solution)/shard_map/attention_backward/pallas_call | solution.py:536
  68.8 1.8 %finish.1 = (bf16[64,2048]{1,0:T(8,128)(2,1)}, bf16[64,512]{1,0:T(8,128)(2,1)}, bf16[64,512]{1,0:T(8,128)(2,1)}) custom-call(bf16[64,2048]{1,0:T(8,128)(2,1)} %get-tuple-element.5.dq_ref, bf16[2,3,64,512]{3,2,1,0:T(8,128)(2,1)} %get-tuple-element.6.dkv_ref), custom_call_target="tpu_custom_call" | custom-call | tf_op jit(solution)/shard_map/finish/pallas_call | solution.py:580

commit v5 on v4

--- a/solution.py
+++ b/solution.py
@@ -24,8 +24,8 @@
     (2, 0), (0, 2), (2, -1), (2, 1), (-1, 2), (1, 2), (2, 2),
 )
 FAR_FIRST = (
-    (2, 2), (1, 2), (-1, 2), (2, 1), (2, -1), (0, 2), (2, 0), (0, 1), (0, -1), (1, 0), (-1, 0),
-    (1, 1), (1, -1), (-1, 1), (-1, -1), (0, 0),
+    (2, 2), (1, 2), (-1, 2), (2, 1), (2, -1), (0, 2), (2, 0), (1, 1), (1, -1), (-1, 1), (-1, -1),
+    (0, 1), (0, -1), (1, 0), (-1, 0), (0, 0),
 )
 
 
@@ -199,19 +199,20 @@
                 arrived(half(firsts[k], second, h), first_recv.at[2 + h])
         spread(k)
 
+    second_odd = lax.rem(second, 2)
+    onward, behind = wrap(second + 1 - 2 * second_odd), wrap(second - 1 + 2 * second_odd)
+
     def second_hop(k):
         i = firsts[k]
-        arrived(block(i, left), second_recv.at[k, 0])
-        relay(half(i, left, 0), (second_send.at[k, 2], second_recv.at[k, 2]), target(first, right))
+        arrived(block(i, behind), second_recv.at[k, second_odd])
+        relay(block(i, behind), (second_send.at[k, 2], second_recv.at[k, 2]), target(first, onward))
+        arrived(block(i, onward), second_recv.at[k, 1 - second_odd])
         share(i, left, steps[k], -1)
-        arrived(block(i, right), second_recv.at[k, 1])
-        relay(half(i, right, 1), (second_send.at[k, 3], second_recv.at[k, 3]), target(first, left))
         share(i, right, steps[k], 1)
 
     def last_hop(k):
         i, j = firsts[k], wrap(second + 2)
-        arrived(half(i, j, 0), second_recv.at[k, 2])
-        arrived(half(i, j, 1), second_recv.at[k, 3])
+        arrived(block(i, j), second_recv.at[k, 2])
         share(i, j, steps[k], 2)
 
     def queries_here():
@@ -403,9 +404,10 @@
         5: (lambda: ring_one(1),),
         6: (lambda: ring_two(3),),
         7: (lambda: ring_one(0),),
-        11: (lambda: ring_two(0), lambda: home(3)),
-        14: (lambda: ring_two(2),),
-        15: (lambda: ring_two(1),),
+        10: (lambda: ring_two(2),),
+        11: (lambda: ring_two(1),),
+        12: (lambda: home(3),),
+        15: (lambda: ring_two(0),),
     }
 
     def backward_step(n, b):
@@ -441,7 +443,6 @@
 
     over_blocks(FAR_FIRST, backward_step)
 
-    home(0)
     for s in range(2):
         for h in range(PER_GROUP):
             dq_own[s, :, pl.ds(h * 128, 128)] = (
@@ -459,6 +460,7 @@
         )
     home(2)
     home(1)
+    home(0)
 
     for role in range(2):
         for a in range(3):
@@ -483,9 +485,9 @@
     for k in range(4):
         for h in range(2):
             arrived(whole, second_send.at[k, h])
-            arrived(halved, second_send.at[k, 2 + h])
             arrived(halved, ring_send.at[k, h])
             arrived(whole, ring_send.at[k, 2 + h])
+        arrived(whole, second_send.at[k, 2])
     for n in range(16):
         arrived(whole, twin_send.at[n])
         arrived(whole, back_send.at[n])
@@ -564,7 +566,7 @@
             DMA((2, 4)), DMA((4, 2)),
             DMA((2, 4)), DMA((2, 4)),
             DMA((4,)), DMA((4,)),
-            DMA((4, 4)), DMA((4, 4)),
+            DMA((4, 3)), DMA((4, 3)),
             DMA((16,)), DMA((16,)),
             DMA((16,)), DMA((16,)),
             DMA((4, 4)), DMA((4, 4)),

time: 70.8 us -> 67.6 us (0.955)
  the two profiles are of different devices: /device:TPU:3 before, /device:TPU:1 now
where the time goes in v5:
time: 67.6 us; the launch traced here: 67.2 us
  Pallas kernels  66.6 us (99%)
    pallas_call x1, Pallas kernels, body(): pl.pallas_call(kernel, out_shape=(jax.ShapeDtypeStruct((64, 2048), BF16),...  64.7 us
    pallas_call x1, Pallas kernels, body(): pl.pallas_call(finish_kernel, out_shape=(jax.ShapeDtypeStruct((64, 2048),...  1.84 us

profile of v5, /device:TPU:1, one launch (start us, length us, event | category | flops | bytes accessed | tf_op | source)
XLA Modules:
  0.0 67.2 jit_solution(679217041719452946)
XLA Ops:
  0.6 64.7 %attention_backward.1 = (bf16[64,2048]{1,0:T(8,128)(2,1)}, bf16[2,3,64,512]{3,2,1,0:T(8,128)(2,1)}) custom-call(s32[64,128]{1,0:T(8,128)} %bitcast.1, bf16[64,2048]{1,0:T(8,128)(2,1)} %q_ref.1, bf16[64,512]{1,0:T(8,128)(2,1)} %k_ref.1, bf16[64,512]{1,0:T(8,128)(2,1)} %v_ref.1, bf16[64,2048]{1,0:T(8,128)(2,1)} %o_ref.1), custom_call_target="tpu_custom_call" | custom-call | tf_op jit(solution)/shard_map/attention_backward/pallas_call | solution.py:538
  65.4 1.8 %finish.1 = (bf16[64,2048]{1,0:T(8,128)(2,1)}, bf16[64,512]{1,0:T(8,128)(2,1)}, bf16[64,512]{1,0:T(8,128)(2,1)}) custom-call(bf16[64,2048]{1,0:T(8,128)(2,1)} %get-tuple-element.5.dq_ref, bf16[2,3,64,512]{3,2,1,0:T(8,128)(2,1)} %get-tuple-element.6.dkv_ref), custom_call_target="tpu_custom_call" | custom-call | tf_op jit(solution)/shard_map/finish/pallas_call | solution.py:582

commit v6 on v4

--- a/solution.py
+++ b/solution.py
@@ -12,7 +12,7 @@
 TILE = 256
 PER_GROUP = 4
 ROWS = PER_GROUP * CHUNK
-ITEMS = 33
+ITEMS = 48
 HIDDEN = -1e30
 FACTOR = HEAD_SIZE**-0.5
 BF16 = jnp.bfloat16
@@ -24,8 +24,8 @@
     (2, 0), (0, 2), (2, -1), (2, 1), (-1, 2), (1, 2), (2, 2),
 )
 FAR_FIRST = (
-    (2, 2), (1, 2), (-1, 2), (2, 1), (2, -1), (0, 2), (2, 0), (0, 1), (0, -1), (1, 0), (-1, 0),
-    (1, 1), (1, -1), (-1, 1), (-1, -1), (0, 0),
+    (2, 2), (1, 2), (-1, 2), (2, 1), (2, -1), (0, 2), (2, 0), (1, 1), (1, -1), (-1, 1), (-1, -1),
+    (0, 1), (0, -1), (1, 0), (-1, 0), (0, 0),
 )
 
 
@@ -59,7 +59,6 @@
         if r:
             others.append(device(x, y, other_z, core))
         others.append(device(x, y, other_z, 1 - core))
-        others.append(device(3 - x, 3 - y, other_z, 1 - core))
     for step in (-1, 1):
         others.append(device(wrap(x + step), y, z, core))
         others.append(device(x, wrap(y + step), z, core))
@@ -104,9 +103,7 @@
         return device(i + core * (j - i), j + core * (i - j), z, core)
 
     other_core = device(x, y, z, 1 - core)
-    odd = lax.rem(z, 2)
-    my_part = part + odd * (31 - 2 * part)
-    my_block = lax.div(my_part, 2)
+    my_block = lax.div(part, 2)
 
     greet(x, y, z, core)
 
@@ -137,15 +134,14 @@
     own_rows = pl.ds(pl.multiple_of(z_lo * 64, 64), 64)
     for r in (2, 1, 3, 0):
         other_z = lax.rem(z + r, 4)
-        flip = lax.rem(z_hi + other_z, 2)
-        to = device(x + flip * (3 - 2 * x), y + flip * (3 - 2 * y), other_z, core + flip * (1 - 2 * core))
+        to = device(x, y, other_z, core)
         columns = pl.ds(pl.multiple_of(other_z * 512, 512), 512)
         for role, ref in ((0, q_ref), (1, o_ref)):
             args = (ref.at[:, columns], landed.at[role, z_hi, own_rows], qo_send.at[role, r], qo_recv.at[role, z])
             if r:
                 go(*args, to)
             else:
-                go_or_keep(flip == 0, *args, to)
+                pltpu.make_async_copy(args[0], args[1], args[3]).start()
 
     up, down = wrap(first + 1), wrap(first - 1)
     left, right = wrap(second - 1), wrap(second + 1)
@@ -228,16 +224,15 @@
                 os[s, lines, :] = landed[1, s, :, lanes]
 
     gather_events = {
-        0: (begin, queries_here),
-        1: (lambda: first_hop(1), lambda: first_hop(2), lambda: second_hop(0)),
-        3: (lambda: first_hop(3),),
-        5: (lambda: second_hop(1),),
-        6: (lambda: second_hop(2),),
-        7: (lambda: last_hop(0),),
-        8: (lambda: second_hop(3),),
-        10: (lambda: last_hop(1),),
-        11: (lambda: last_hop(2),),
-        12: (lambda: last_hop(3),),
+        0: (begin, lambda: first_hop(1), lambda: first_hop(2), queries_here),
+        1: (lambda: second_hop(0), lambda: first_hop(3)),
+        3: (lambda: second_hop(1),),
+        4: (lambda: second_hop(2),),
+        6: (lambda: last_hop(0),),
+        7: (lambda: second_hop(3),),
+        9: (lambda: last_hop(1),),
+        10: (lambda: last_hop(2),),
+        11: (lambda: last_hop(3),),
     }
 
     def run(events, n):
@@ -263,8 +258,8 @@
         lax.fori_loop(0, 16, turn, (start_x + 0 * x, start_y + 0 * x))
 
     def in_full(b, work):
-        kind = at_most(b, my_block) + 2 * at_most(b, 15 - my_block)
-        for number in range(4):
+        kind = 3 * at_most(b, my_block)
+        for number in (0, 3):
 
             @pl.when(kind == number)
             def _():
@@ -274,7 +269,7 @@
         return (0, 1) if s and with_late else (0,)
 
     def number_of(b, s, late):
-        return (32 - b) if late else b + 16 * (1 - s)
+        return (32 + b) if late else b + 16 * (1 - s)
 
     scale = FACTOR * math.log2(math.e)
     top[...] = jnp.full(top.shape, HIDDEN, F32)
@@ -298,7 +293,7 @@
                 for late in range(1 + with_late)
             ]
             for s in (1, 0) if with_a else (1,):
-                chunk = my_part if s == 0 else 63 - my_part
+                chunk = part + 32 * s
                 query_pos = chunk * CHUNK + lax.broadcasted_iota(jnp.int32, (1, CHUNK), 1)
                 query_turn = turn_ref[pl.ds(chunk, 1), :]
                 old_top = top[s]
@@ -403,9 +398,10 @@
         5: (lambda: ring_one(1),),
         6: (lambda: ring_two(3),),
         7: (lambda: ring_one(0),),
-        11: (lambda: ring_two(0), lambda: home(3)),
-        14: (lambda: ring_two(2),),
-        15: (lambda: ring_two(1),),
+        10: (lambda: ring_two(2),),
+        11: (lambda: ring_two(1),),
+        12: (lambda: home(3),),
+        15: (lambda: ring_two(0),),
     }
 
     def backward_step(n, b):
@@ -441,7 +437,6 @@
 
     over_blocks(FAR_FIRST, backward_step)
 
-    home(0)
     for s in range(2):
         for h in range(PER_GROUP):
             dq_own[s, :, pl.ds(h * 128, 128)] = (
@@ -449,16 +444,16 @@
             ).astype(BF16)
     for other_z in range(4):
         s = other_z // 2
-        flip = lax.rem(s + odd, 2)
-        to = device(x + flip * (3 - 2 * x), y + flip * (3 - 2 * y), other_z, core + flip * (1 - 2 * core))
+        to = device(x, y, other_z, core)
         go_or_keep(
-            (flip == 0) & (z == other_z),
+            z == other_z,
             dq_own.at[s, pl.ds((other_z % 2) * 64, 64)],
             dq_out.at[:, pl.ds(pl.multiple_of(z * 512, 512), 512)],
             dq_send.at[other_z], dq_recv.at[z], to,
         )
     home(2)
     home(1)
+    home(0)
 
     for role in range(2):
         for a in range(3):
@@ -498,11 +493,6 @@
     def _():
         arrived(k_ref.at[:, pl.ds(0, 128)], kv_send.at[0, 0])
 
-    @pl.when(lax.rem(z_hi + z_lo, 2) == 1)
-    def _():
-        for role in range(2):
-            arrived(q_ref.at[:, pl.ds(0, 512)], qo_send.at[role, 0])
-
     for other_z in range(4):
         for c in range(2):
 
@@ -510,9 +500,7 @@
             def _():
                 arrived(piece, last_send.at[0, other_z, c])
 
-        flip = lax.rem(other_z // 2 + odd, 2)
-
-        @pl.when(jnp.logical_not((flip == 0) & (z == other_z)))
+        @pl.when(z != other_z)
         def _():
             arrived(dq_own.at[0, pl.ds(0, 64)], dq_send.at[other_z])
 

time: 70.8 us -> 66.4 us (0.938)
  the two profiles are of different devices: /device:TPU:3 before, /device:TPU:7 now
where the time goes in v6:
time: 66.4 us; the launch traced here: 66.2 us
  Pallas kernels  65.5 us (99%)
    pallas_call x1, Pallas kernels, body(): pl.pallas_call(kernel, out_shape=(jax.ShapeDtypeStruct((64, 2048), BF16),...  63.7 us
    pallas_call x1, Pallas kernels, body(): pl.pallas_call(finish_kernel, out_shape=(jax.ShapeDtypeStruct((64, 2048),...  1.84 us

profile of v6, /device:TPU:7, one launch (start us, length us, event | category | flops | bytes accessed | tf_op | source)
XLA Modules:
  0.0 66.2 jit_solution(1659433687648909122)
XLA Ops:
  0.6 63.7 %attention_backward.1 = (bf16[64,2048]{1,0:T(8,128)(2,1)}, bf16[2,3,64,512]{3,2,1,0:T(8,128)(2,1)}) custom-call(s32[64,128]{1,0:T(8,128)} %bitcast.1, bf16[64,2048]{1,0:T(8,128)(2,1)} %q_ref.1, bf16[64,512]{1,0:T(8,128)(2,1)} %k_ref.1, bf16[64,512]{1,0:T(8,128)(2,1)} %v_ref.1, bf16[64,2048]{1,0:T(8,128)(2,1)} %o_ref.1), custom_call_target="tpu_custom_call" | custom-call | tf_op jit(solution)/shard_map/attention_backward/pallas_call | solution.py:524
  64.3 1.8 %finish.1 = (bf16[64,2048]{1,0:T(8,128)(2,1)}, bf16[64,512]{1,0:T(8,128)(2,1)}, bf16[64,512]{1,0:T(8,128)(2,1)}) custom-call(bf16[64,2048]{1,0:T(8,128)(2,1)} %get-tuple-element.5.dq_ref, bf16[2,3,64,512]{3,2,1,0:T(8,128)(2,1)} %get-tuple-element.6.dkv_ref), custom_call_target="tpu_custom_call" | custom-call | tf_op jit(solution)/shard_map/finish/pallas_call | solution.py:568

commit v7 on v6

--- a/solution.py
+++ b/solution.py
@@ -12,7 +12,6 @@
 TILE = 256
 PER_GROUP = 4
 ROWS = PER_GROUP * CHUNK
-ITEMS = 48
 HIDDEN = -1e30
 FACTOR = HEAD_SIZE**-0.5
 BF16 = jnp.bfloat16
@@ -79,7 +78,7 @@
 
 def kernel(
     turn_ref, q_ref, k_ref, v_ref, o_ref, dq_out, last,
-    kv, landed, qs, os, weights, probs_grad, tile_max, top, total, dot, dq_acc, dq_own,
+    kv, landed, qs, os, weights_b, weights_a, grads_b, grads_a, tile_max, top, total, dot, dq_acc, dq_own,
     partial, twin, sums, one, two, line, line_in,
     kv_send, kv_recv, qo_send, qo_recv, first_send, first_recv, second_send, second_recv,
     twin_send, twin_recv, back_send, back_recv, ring_send, ring_recv, last_send, last_recv,
@@ -265,11 +264,14 @@
             def _():
                 work(number % 2, number // 2)
 
-    def tiles_of(s, with_late):
-        return (0, 1) if s and with_late else (0,)
-
-    def number_of(b, s, late):
-        return (32 + b) if late else b + 16 * (1 - s)
+    def groups(with_a, with_late):
+        return ((1, TILE * (1 + with_late)),) + ((0, TILE),) * with_a
+
+    def held(ref_b, ref_a, b, s, count):
+        return ref_b.at[b, pl.ds(0, count)] if s else ref_a.at[b]
+
+    def keys_of(b, role, count):
+        return kv[role, b].reshape(2 * TILE, HEAD_SIZE) if count > TILE else kv[role, b, 0]
 
     scale = FACTOR * math.log2(math.e)
     top[...] = jnp.full(top.shape, HIDDEN, F32)
@@ -282,54 +284,44 @@
         arrived(kv.at[1 - core, b], twin_recv.at[n])
 
         def stats(with_a, with_late):
-            key_turns = [
-                jnp.concatenate(
-                    [
-                        jnp.broadcast_to(turn_ref[pl.ds(2 * (late * 16 + b) + i, 1), :], (128, 128)).T
-                        for i in range(2)
-                    ],
-                    axis=0,
+            count = TILE * (1 + with_late)
+            key_turns = jnp.concatenate(
+                [
+                    jnp.broadcast_to(turn_ref[pl.ds(2 * (late * 16 + b) + i, 1), :], (128, 128)).T
+                    for late in range(1 + with_late)
+                    for i in range(2)
+                ],
+                axis=0,
+            )
+            row = lax.broadcasted_iota(jnp.int32, (count, CHUNK), 0)
+            key_places = b * TILE + row + jnp.where(row >= TILE, 15 * TILE, 0)
+            parts = []
+            for s, count in groups(with_a, with_late):
+                query_pos = (part + 32 * s) * CHUNK + lax.broadcasted_iota(jnp.int32, (1, CHUNK), 1)
+                query_turn = turn_ref[pl.ds(part + 32 * s, 1), :]
+                key_turn, key_pos = key_turns[:count], key_places[:count]
+                visible = (key_pos <= query_pos) & (
+                    (key_turn == query_turn) | ((key_turn & 1) == 0)
                 )
-                for late in range(1 + with_late)
-            ]
-            for s in (1, 0) if with_a else (1,):
-                chunk = part + 32 * s
-                query_pos = chunk * CHUNK + lax.broadcasted_iota(jnp.int32, (1, CHUNK), 1)
-                query_turn = turn_ref[pl.ds(chunk, 1), :]
+                logits = lax.dot_general(
+                    keys_of(b, 0, count), qs[s], (((1,), (1,)), ((), ())), preferred_element_type=F32
+                )
+                grads = lax.dot_general(
+                    keys_of(b, 1, count), os[s], (((1,), (1,)), ((), ())), preferred_element_type=F32
+                )
+                bias = jnp.where(visible, 0.0, HIDDEN)
+                parts.append((s, count, logits * scale + jnp.concatenate([bias] * PER_GROUP, axis=1), grads))
+            for s, count, logits, grads in parts:
                 old_top = top[s]
-                new_top = old_top
-                parts = []
-                for late in tiles_of(s, with_late):
-                    key_turn = key_turns[late]
-                    key_pos = (late * 16 + b) * TILE + lax.broadcasted_iota(
-                        jnp.int32, (TILE, CHUNK), 0
-                    )
-                    visible = (key_pos <= query_pos) & (
-                        (key_turn == query_turn) | ((key_turn & 1) == 0)
-                    )
-                    logits = lax.dot_general(
-                        kv[0, b, late], qs[s], (((1,), (1,)), ((), ())), preferred_element_type=F32
-                    )
-                    bias = jnp.where(visible, 0.0, HIDDEN)
-                    logits = logits * scale + jnp.concatenate([bias] * PER_GROUP, axis=1)
-                    new_top = jnp.maximum(new_top, jnp.max(logits, axis=0, keepdims=True))
-                    grads = lax.dot_general(
-                        kv[1, b, late], os[s], (((1,), (1,)), ((), ())), preferred_element_type=F32
-                    )
-                    parts.append((late, logits, grads))
+                new_top = jnp.maximum(old_top, jnp.max(logits, axis=0, keepdims=True))
                 shrink = jnp.exp2(old_top - new_top)
-                new_total, new_dot = total[s] * shrink, dot[s] * shrink
-                for late, logits, grads in parts:
-                    number = number_of(b, s, late)
-                    weight = jnp.exp2(logits - new_top)
-                    weights[number] = weight.astype(BF16)
-                    probs_grad[number] = grads.astype(BF16)
-                    tile_max[number] = new_top
-                    new_total += jnp.sum(weight, axis=0, keepdims=True)
-                    new_dot += jnp.sum(weight * grads, axis=0, keepdims=True)
+                weight = jnp.exp2(logits - new_top)
+                held(weights_b, weights_a, b, s, count)[...] = weight.astype(BF16)
+                held(grads_b, grads_a, b, s, count)[...] = grads.astype(BF16)
+                tile_max[s, b] = new_top
                 top[s] = new_top
-                total[s] = new_total
-                dot[s] = new_dot
+                total[s] = total[s] * shrink + jnp.sum(weight, axis=0, keepdims=True)
+                dot[s] = dot[s] * shrink + jnp.sum(weight * grads, axis=0, keepdims=True)
 
         in_full(b, stats)
 
@@ -406,30 +398,28 @@
 
     def backward_step(n, b):
         def terms(with_a, with_late):
-            keys_sum, values_sum = [0.0, 0.0], [0.0, 0.0]
-            for s in (1, 0) if with_a else (1,):
-                query_sum = dq_acc[s]
-                for late in tiles_of(s, with_late):
-                    number = number_of(b, s, late)
-                    by = jnp.exp2(tile_max[number] - top[s]) * total[s]
-                    attention = weights[number].astype(F32) * by
-                    logit_grad = (attention * (probs_grad[number].astype(F32) - dot[s])).astype(BF16)
-                    values_sum[late] += jnp.dot(
-                        attention.astype(BF16), os[s], preferred_element_type=F32
-                    )
-                    keys_sum[late] += jnp.dot(logit_grad, qs[s], preferred_element_type=F32)
-                    query_sum += lax.dot_general(
-                        logit_grad, kv[0, b, late], (((0,), (0,)), ((), ())),
-                        preferred_element_type=F32,
-                    )
-                dq_acc[s] = query_sum
-            for late in range(2):
-                if late <= with_late:
-                    partial[0, b, late] = (keys_sum[late] * FACTOR).astype(BF16)
-                    partial[1, b, late] = values_sum[late].astype(BF16)
+            sums_of = []
+            for s, count in groups(with_a, with_late):
+                by = jnp.exp2(tile_max[s, b] - top[s]) * total[s]
+                attention = held(weights_b, weights_a, b, s, count)[...].astype(F32) * by
+                grads = held(grads_b, grads_a, b, s, count)[...].astype(F32)
+                logit_grad = (attention * (grads - dot[s])).astype(BF16)
+                value_sum = jnp.dot(attention.astype(BF16), os[s], preferred_element_type=F32)
+                key_sum = jnp.dot(logit_grad, qs[s], preferred_element_type=F32)
+                dq_acc[s] += lax.dot_general(
+                    logit_grad, keys_of(b, 0, count), (((0,), (0,)), ((), ())),
+                    preferred_element_type=F32,
+                )
+                sums_of.append((key_sum * FACTOR, value_sum))
+            for role in range(2):
+                early = sums_of[0][role][:TILE]
+                if with_a:
+                    early = early + sums_of[1][role]
+                partial[role, b, 0] = early.astype(BF16)
+                if with_late:
+                    partial[role, b, 1] = sums_of[0][role][TILE:].astype(BF16)
                 else:
-                    partial[0, b, late] = jnp.zeros((TILE, HEAD_SIZE), BF16)
-                    partial[1, b, late] = jnp.zeros((TILE, HEAD_SIZE), BF16)
+                    partial[role, b, 1] = jnp.zeros((TILE, HEAD_SIZE), BF16)
 
         in_full(b, terms)
         send(partial.at[1 - core, b], twin.at[b], back_send.at[n], back_recv.at[n], other_core).start()
@@ -534,9 +524,11 @@
             pltpu.VMEM((2, 2, CHUNK, 512), BF16),
             pltpu.VMEM((2, ROWS, HEAD_SIZE), BF16),
             pltpu.VMEM((2, ROWS, HEAD_SIZE), BF16),
-            pltpu.VMEM((ITEMS, TILE, ROWS), BF16),
-            pltpu.VMEM((ITEMS, TILE, ROWS), BF16),
-            pltpu.VMEM((ITEMS, 1, ROWS), F32),
+            pltpu.VMEM((16, 2 * TILE, ROWS), BF16),
+            pltpu.VMEM((16, TILE, ROWS), BF16),
+            pltpu.VMEM((16, 2 * TILE, ROWS), BF16),
+            pltpu.VMEM((16, TILE, ROWS), BF16),
+            pltpu.VMEM((2, 16, 1, ROWS), F32),
             pltpu.VMEM((2, 1, ROWS), F32),
             pltpu.VMEM((2, 1, ROWS), F32),
             pltpu.VMEM((2, 1, ROWS), F32),

time: 66.4 us -> 65.4 us (0.985)
  Pallas kernels: 65.5 us -> 64.5 us
    pallas_call x1, Pallas kernels: 63.7 us -> 62.7 us  [body(): pl.pallas_call(kernel, out_shape=(jax.ShapeDtypeStruct((64, 2048), BF16),...]
where the time goes in v7:
time: 65.4 us; the launch traced here: 65.1 us
  Pallas kernels  64.5 us (99%)
    pallas_call x1, Pallas kernels, body(): pl.pallas_call(kernel, out_shape=(jax.ShapeDtypeStruct((64, 2048), BF16),...  62.7 us
    pallas_call x1, Pallas kernels, body(): pl.pallas_call(finish_kernel, out_shape=(jax.ShapeDtypeStruct((64, 2048),...  1.84 us

profile of v7, /device:TPU:7, one launch (start us, length us, event | category | flops | bytes accessed | tf_op | source)
XLA Modules:
  0.0 65.1 jit_solution(12987873796720924676)
XLA Ops:
  0.6 62.7 %attention_backward.1 = (bf16[64,2048]{1,0:T(8,128)(2,1)}, bf16[2,3,64,512]{3,2,1,0:T(8,128)(2,1)}) custom-call(s32[64,128]{1,0:T(8,128)} %bitcast.1, bf16[64,2048]{1,0:T(8,128)(2,1)} %q_ref.1, bf16[64,512]{1,0:T(8,128)(2,1)} %k_ref.1, bf16[64,512]{1,0:T(8,128)(2,1)} %v_ref.1, bf16[64,2048]{1,0:T(8,128)(2,1)} %o_ref.1), custom_call_target="tpu_custom_call" | custom-call | tf_op jit(solution)/shard_map/attention_backward/pallas_call | solution.py:514
  63.3 1.8 %finish.1 = (bf16[64,2048]{1,0:T(8,128)(2,1)}, bf16[64,512]{1,0:T(8,128)(2,1)}, bf16[64,512]{1,0:T(8,128)(2,1)}) custom-call(bf16[64,2048]{1,0:T(8,128)(2,1)} %get-tuple-element.5.dq_ref, bf16[2,3,64,512]{3,2,1,0:T(8,128)(2,1)} %get-tuple-element.6.dkv_ref), custom_call_target="tpu_custom_call" | custom-call | tf_op jit(solution)/shard_map/finish/pallas_call | solution.py:560

commit v8 on v7

--- a/solution.py
+++ b/solution.py
@@ -77,12 +77,12 @@
 
 
 def kernel(
-    turn_ref, q_ref, k_ref, v_ref, o_ref, dq_out, last,
-    kv, landed, qs, os, weights_b, weights_a, grads_b, grads_a, tile_max, top, total, dot, dq_acc, dq_own,
+    turns, q_ref, k_ref, v_ref, o_ref, dq_out, last,
+    turn_ref, kv, landed, qs, os, weights_b, weights_a, grads_b, grads_a, tile_max, top, total, dot, dq_acc, dq_own,
     partial, twin, sums, one, two, line, line_in,
     kv_send, kv_recv, qo_send, qo_recv, first_send, first_recv, second_send, second_recv,
     twin_send, twin_recv, back_send, back_recv, ring_send, ring_recv, last_send, last_recv,
-    line_send, line_recv,     dq_send, dq_recv,
+    line_send, line_recv,     dq_send, dq_recv, turn_sem,
 ):
     blk = lax.axis_index("blk")
     z_lo = lax.axis_index("head")
@@ -104,6 +104,7 @@
     other_core = device(x, y, z, 1 - core)
     my_block = lax.div(part, 2)
 
+    pltpu.make_async_copy(turns, turn_ref, turn_sem).start()
     greet(x, y, z, core)
 
     def go(src, dst, send_sem, recv_sem, to):
@@ -210,6 +211,7 @@
         share(i, j, steps[k], 2)
 
     def queries_here():
+        arrived(turn_ref, turn_sem)
         for role in range(2):
             for other_z in range(4):
                 arrived(
@@ -306,16 +308,16 @@
                 logits = lax.dot_general(
                     keys_of(b, 0, count), qs[s], (((1,), (1,)), ((), ())), preferred_element_type=F32
                 )
-                grads = lax.dot_general(
-                    keys_of(b, 1, count), os[s], (((1,), (1,)), ((), ())), preferred_element_type=F32
-                )
                 bias = jnp.where(visible, 0.0, HIDDEN)
-                parts.append((s, count, logits * scale + jnp.concatenate([bias] * PER_GROUP, axis=1), grads))
-            for s, count, logits, grads in parts:
+                parts.append((s, count, logits * scale + jnp.concatenate([bias] * PER_GROUP, axis=1)))
+            for s, count, logits in parts:
                 old_top = top[s]
                 new_top = jnp.maximum(old_top, jnp.max(logits, axis=0, keepdims=True))
                 shrink = jnp.exp2(old_top - new_top)
                 weight = jnp.exp2(logits - new_top)
+                grads = lax.dot_general(
+                    keys_of(b, 1, count), os[s], (((1,), (1,)), ((), ())), preferred_element_type=F32
+                )
                 held(weights_b, weights_a, b, s, count)[...] = weight.astype(BF16)
                 held(grads_b, grads_a, b, s, count)[...] = grads.astype(BF16)
                 tile_max[s, b] = new_top
@@ -517,9 +519,10 @@
             jax.ShapeDtypeStruct((64, 2048), BF16),
             jax.ShapeDtypeStruct((2, 3, 64, 512), BF16),
         ),
-        in_specs=[VMEM] + [ANY] * 4,
+        in_specs=[ANY] * 5,
         out_specs=(ANY, ANY),
         scratch_shapes=[
+            pltpu.VMEM((64, CHUNK), jnp.int32),
             pltpu.VMEM((2, 16) + block, BF16),
             pltpu.VMEM((2, 2, CHUNK, 512), BF16),
             pltpu.VMEM((2, ROWS, HEAD_SIZE), BF16),
@@ -551,6 +554,7 @@
             DMA((3, 4, 2)), DMA((2, 3, 4)),
             DMA((2,)), DMA((2,)),
             DMA((4,)), DMA((4,)),
+            DMA,
         ],
         compiler_params=pltpu.CompilerParams(
             collective_id=0, has_side_effects=True, vmem_limit_bytes=58 << 20

time: 65.4 us -> 63.9 us (0.977)
  the two profiles are of different devices: /device:TPU:7 before, /device:TPU:1 now
where the time goes in v8:
time: 63.9 us; the launch traced here: 62.8 us
  Pallas kernels  62.2 us (97%)
  between operations  0.64 us (1%)
    pallas_call x1, Pallas kernels, body(): pl.pallas_call(kernel, out_shape=(jax.ShapeDtypeStruct((64, 2048), BF16),...  60.4 us
    pallas_call x1, Pallas kernels, body(): pl.pallas_call(finish_kernel, out_shape=(jax.ShapeDtypeStruct((64, 2048),...  1.84 us

profile of v8, /device:TPU:1, one launch (start us, length us, event | category | flops | bytes accessed | tf_op | source)
XLA Modules:
  0.0 62.8 jit_solution(5163455950124706438)
XLA Ops:
  0.6 60.4 %attention_backward.1 = (bf16[64,2048]{1,0:T(8,128)(2,1)}, bf16[2,3,64,512]{3,2,1,0:T(8,128)(2,1)}) custom-call(s32[64,128]{1,0:T(8,128)} %bitcast.1, bf16[64,2048]{1,0:T(8,128)(2,1)} %q_ref.1, bf16[64,512]{1,0:T(8,128)(2,1)} %k_ref.1, bf16[64,512]{1,0:T(8,128)(2,1)} %v_ref.1, bf16[64,2048]{1,0:T(8,128)(2,1)} %o_ref.1), custom_call_target="tpu_custom_call" | custom-call | tf_op jit(solution)/shard_map/attention_backward/pallas_call | solution.py:516
  61.0 1.8 %finish.1 = (bf16[64,2048]{1,0:T(8,128)(2,1)}, bf16[64,512]{1,0:T(8,128)(2,1)}, bf16[64,512]{1,0:T(8,128)(2,1)}) custom-call(bf16[64,2048]{1,0:T(8,128)(2,1)} %get-tuple-element.5.dq_ref, bf16[2,3,64,512]{3,2,1,0:T(8,128)(2,1)} %get-tuple-element.6.dkv_ref), custom_call_target="tpu_custom_call" | custom-call | tf_op jit(solution)/shard_map/finish/pallas_call | solution.py:564

commit v9 on v8

--- a/solution.py
+++ b/solution.py
@@ -390,11 +390,10 @@
         1: (lambda: ring_one(3),),
         4: (lambda: ring_one(2),),
         5: (lambda: ring_one(1),),
-        6: (lambda: ring_two(3),),
-        7: (lambda: ring_one(0),),
-        10: (lambda: ring_two(2),),
-        11: (lambda: ring_two(1),),
-        12: (lambda: home(3),),
+        7: (lambda: ring_one(0), lambda: ring_two(3)),
+        11: (lambda: ring_two(2),),
+        12: (lambda: ring_two(1),),
+        13: (lambda: home(3),),
         15: (lambda: ring_two(0),),
     }
 

time: 63.9 us -> 63.3 us (level)
  no operation moved by 1% of the time
where the time goes in v9:
time: 63.3 us; the launch traced here: 62.7 us
  Pallas kernels  62.1 us (98%)
  between operations  0.64 us (1%)
    pallas_call x1, Pallas kernels, body(): pl.pallas_call(kernel, out_shape=(jax.ShapeDtypeStruct((64, 2048), BF16),...  60.2 us
    pallas_call x1, Pallas kernels, body(): pl.pallas_call(finish_kernel, out_shape=(jax.ShapeDtypeStruct((64, 2048),...  1.84 us

profile of v9, /device:TPU:1, one launch (start us, length us, event | category | flops | bytes accessed | tf_op | source)
XLA Modules:
  0.0 62.7 jit_solution(13582617784649170179)
XLA Ops:
  0.6 60.2 %attention_backward.1 = (bf16[64,2048]{1,0:T(8,128)(2,1)}, bf16[2,3,64,512]{3,2,1,0:T(8,128)(2,1)}) custom-call(s32[64,128]{1,0:T(8,128)} %bitcast.1, bf16[64,2048]{1,0:T(8,128)(2,1)} %q_ref.1, bf16[64,512]{1,0:T(8,128)(2,1)} %k_ref.1, bf16[64,512]{1,0:T(8,128)(2,1)} %v_ref.1, bf16[64,2048]{1,0:T(8,128)(2,1)} %o_ref.1), custom_call_target="tpu_custom_call" | custom-call | tf_op jit(solution)/shard_map/attention_backward/pallas_call | solution.py:515
  60.9 1.8 %finish.1 = (bf16[64,2048]{1,0:T(8,128)(2,1)}, bf16[64,512]{1,0:T(8,128)(2,1)}, bf16[64,512]{1,0:T(8,128)(2,1)}) custom-call(bf16[64,2048]{1,0:T(8,128)(2,1)} %get-tuple-element.5.dq_ref, bf16[2,3,64,512]{3,2,1,0:T(8,128)(2,1)} %get-tuple-element.6.dkv_ref), custom_call_target="tpu_custom_call" | custom-call | tf_op jit(solution)/shard_map/finish/pallas_call | solution.py:563
